TPU v7x, 512 devices: a whole 4x4x16 slice. The times are simulated.
512 devices in a mesh: tx: 4 (over y), ty: 8 (over x, core), depth: 16 (over z).
Axes of the slice: x: 4, y: 4, z: 16, core: 2. Of those that a mesh axis runs over, the one named last changes fastest.
Arguments:
- volume: bfloat16 [512, 2048, 512], P('depth', 'ty', 'tx'), may hold values from -6 to 6
- transfer: float32 [4, 2], replicated, may hold values from -1.5 to 1.5
- ray_start: int32 [16, 2048, 512], P('depth', 'ty', 'tx'), may hold values from 0 to 15
- ray_stop: int32 [16, 2048, 512], P('depth', 'ty', 'tx'), may hold values from 16 to 32
- pattern: int32 [16, 256, 4], P('depth', 'ty', 'tx'), may hold values 0 or 1
- depth_order: int32 [16], replicated, may hold values from 0 to 15, each once
Outputs:
- frame: float32 [4, 2048, 512], P(None, 'ty', 'tx')
Inputs may be any that keep to these rules, and one draw needn't show every extreme that they name: ray_start[s] < ray_stop[s] for every ray and slice. `depth_order`: each slice appears once.
All inputs are finite; a program needn't handle non-finite values. No bound on the sum of `pattern` on one device may be relied on, other than what follows from the above.
Results may differ from a plain program's by a relative error of at most 0.0003.
Values may be sent and summed in bfloat16 or wider, within the bound.
No kernel may reach another device: no remote copies, remote signals or barrier semaphores. Data moves between devices by JAX's collectives and lax.ppermute only.
A program may use at most 64 MiB of HBM per device.

v0:
```python
import jax
import jax.numpy as jnp
from jax import lax
from jax.sharding import PartitionSpec as P


def extended(array, sides, width):
    edges = {}
    for axis, dim in sides:
        count, length = (lax.axis_size(axis), array.shape[dim])
        up = [(i, (i + 1) % count) for i in range(count - 1)]
        last = lax.slice_in_dim(array, length - width, length, axis=dim)
        initial = lax.slice_in_dim(array, 0, width, axis=dim)
        edges[dim] = (
            lax.ppermute(last, axis, up),
            lax.ppermute(initial, axis, [(b, a) for a, b in up]),
        )
    done = []
    for _, dim in sides:
        low, high = edges[dim]
        around = [(width, width) if d in done else (0, 0) for d in range(array.ndim)]
        array = jnp.concatenate([jnp.pad(low, around), array, jnp.pad(high, around)], axis=dim)
        done.append(dim)
    return array


def local_partial(padded, transfer, ray_start, ray_stop, pattern, depth_count):
    samples = padded.shape[0] - 2
    values = padded[1:-1, 1:-1, 1:-1]
    grad_z = (padded[2:, 1:-1, 1:-1] - padded[:-2, 1:-1, 1:-1]) * 0.5
    grad_y = (padded[1:-1, 2:, 1:-1] - padded[1:-1, :-2, 1:-1]) * 0.5
    grad_x = (padded[1:-1, 1:-1, 2:] - padded[1:-1, 1:-1, :-2]) * 0.5
    lit = jnp.abs(0.48 * grad_x + 0.6 * grad_y + 0.64 * grad_z)
    shading = 0.3 + 0.7 * lit / jnp.sqrt(grad_x * grad_x + grad_y * grad_y + grad_z * grad_z + 1.0)
    rows_each = ray_start.shape[0] // pattern.shape[0]
    cols_each = ray_start.shape[1] // pattern.shape[1]
    pattern_full = jnp.repeat(jnp.repeat(pattern, rows_each, axis=0), cols_each, axis=1)
    layers = lax.broadcasted_iota(jnp.int32, (samples, 1, 1), 0)
    active = (layers >= ray_start[None]) & (layers < ray_stop[None]) & (pattern_full[None] > 0)
    density = jax.nn.softplus(transfer[3, 0] * values + transfer[3, 1]) * (
        2.0 / (samples * depth_count)
    )
    opacity = jnp.where(active, 1.0 - jnp.exp(-density), jnp.float32(0.0))
    passed = jnp.cumprod(1.0 - opacity, axis=0)
    prior = jnp.concatenate([jnp.ones_like(passed[:1]), passed[:-1]], axis=0)
    weights = prior * opacity * shading
    tinted = jax.nn.sigmoid(
        transfer[:3, 0][:, None, None, None] * values[None] + transfer[:3, 1][:, None, None, None]
    )
    colors = jnp.sum(weights[None] * tinted, axis=1)
    return jnp.concatenate([colors, passed[-1][None]], axis=0)


def composite(partials, depth_order):
    count = partials.shape[0]

    def step(position, state_pair):
        colors, remain = state_pair
        slice_part = lax.dynamic_index_in_dim(partials, depth_order[position], 0, keepdims=False)
        return (colors + remain[None] * slice_part[:3], remain * slice_part[3])

    start_pair = (
        jnp.zeros((3,) + partials.shape[2:], jnp.float32),
        jnp.ones(partials.shape[2:], jnp.float32),
    )
    colors, remain = lax.fori_loop(0, count, step, start_pair)
    return jnp.concatenate([colors, 1.0 - remain[None]], axis=0)


def shards(volume, transfer, ray_start, ray_stop, pattern, depth_order):
    padded = extended(volume, (("tx", 2), ("ty", 1), ("depth", 0)), 1).astype(jnp.float32)
    depth_count = lax.axis_size("depth")
    stacked = local_partial(padded, transfer, ray_start[0], ray_stop[0], pattern[0], depth_count)[
        None
    ]
    pixel_share = lax.all_to_all(stacked, "depth", split_axis=2, concat_axis=0, tiled=True)
    picture = composite(pixel_share, depth_order)
    return lax.all_gather(picture, "depth", axis=1, tiled=True)


def solution(mesh):
    in_specs = (
        P("depth", "ty", "tx"),
        P(),
        P("depth", "ty", "tx"),
        P("depth", "ty", "tx"),
        P("depth", "ty", "tx"),
        P(),
    )
    out_specs = P(None, "ty", "tx")
    return jax.shard_map(shards, mesh=mesh, in_specs=in_specs, out_specs=out_specs, check_vma=False)
```

profile of v0, /device:TPU:24, one launch (start us, length us, event | category | flops | bytes accessed | tf_op | source)
XLA Modules:
  0.0 199.9 jit_solution(10582260819200057759)
XLA Ops:
  0.0 0.9 fusion.31
  0.9 1.7 collective-permute-start.1
  2.7 1.3 collective-permute-start.4
  4.0 0.9 fusion.30
  4.8 3.8 %collective-permute-start = (bf16[1,256,128]{2,1,0:T(8,128)(2,1)S(1)}, bf16[1,256,128]{2,1,0:T(8,128)(2,1)S(1)}, u32[]{:S(2)}, u32[]{:S(2)}) collective-permute-start(bf16[1,256,128]{2,1,0:T(8,128)(2,1)S(1)} %get-tuple-element.151), channel_id=1, source_target_pairs={{0,1},{1,2},{2,3},{3,4},{4,5},{5,6},{6,7},{7,8},{8,9},{9,10},{10,1... | collective-permute-start | bytes 196616 | tf_op jit(solution)/shard_map/ppermute | solution.py:15
  8.7 1.3 collective-permute-start.5
  10.0 4.4 %fusion.29 = (bf16[32,256,1]{2,1,0:T(8,128)(2,1)}, bf16[32,256,1]{2,1,0:T(8,128)(2,1)S(1)}) fusion(bf16[32,256,128]{2,1,0:T(8,128)(2,1)} %param.8), kind=kLoop, calls=%fused_computation.52 | loop fusion | bytes 65536 | tf_op jit(solution)/shard_map/slice | solution.py:12
  14.4 2.0 copy.23
  16.3 1.3 collective-permute-start.2
  17.7 0.9 copy.24
  18.6 3.4 %collective-permute-done.2 = bf16[32,256,1]{1,0,2:T(8,128)(2,1)S(1)} collective-permute-done((bf16[32,256,1]{1,0,2:T(8,128)(2,1)S(1)}, bf16[32,256,1]{1,0,2:T(8,128)(2,1)S(1)}, u32[]{:S(2)}, u32[]{:S(2)}) %collective-permute-start.2) | collective-permute-done | bytes 16416 | tf_op jit(solution)/shard_map/ppermute | solution.py:15
  22.0 2.6 %collective-permute-start.3 = (bf16[32,256,1]{1,0,2:T(8,128)(2,1)S(1)}, bf16[32,256,1]{1,0,2:T(8,128)(2,1)S(1)}, u32[]{:S(2)}, u32[]{:S(2)}) collective-permute-start(bf16[32,256,1]{1,0,2:T(8,128)(2,1)S(1)} %copy.24), channel_id=1, source_target_pairs={{128,0},{256,128},{384,256},{129,1},{257,129},{385,257},{130,2},{2... | collective-permute-start | bytes 49160 | tf_op jit(solution)/shard_map/ppermute | solution.py:16
  25.4 1.9 copy.17
  27.3 1.8 copy.18
  29.2 17.7 %fusion.11 = f32[34,258,130]{2,1,0:T(8,128)S(1)} fusion(bf16[1,256,128]{2,1,0:T(8,128)(2,1)S(1)} %collective-permute-done.5, bf16[32,1,128]{2,1,0:T(2,128)(2,1)S(1)} %collective-permute-done.4, bf16[32,1,128]{2,1,0:T(2,128)(2,1)S(1)} %collective-permute-done.1, bf16[1,256,128]{2,1,0:T(8,128)(2,1)S(1)} %collective-permute-done, bf16[32,256,1]{2,1,0:T(8,128)(2,1)} %copy.18, ...), kind=kLoop, calls=%fused_computation.23 | loop fusion | flops 33070440 | bytes 6838816 | tf_op jit(solution)/shard_map/convert_element_type | solution.py:71
  46.9 7.6 %fusion.22 = f32[32,256,128]{2,1,0:T(8,128)} fusion(f32[]{:T(128)} %bitcast.4, f32[]{:T(128)} %bitcast.3, s32[256,128]{1,0:T(8,128)S(1)} %bitcast.41, s32[256,128]{1,0:T(8,128)S(1)} %bitcast.43, pred[256]{0:T(512)(128)(4,1)S(1)} %gt.22, f32[34,258,130]{2,1,0:T(8,128)S(1)} %fusion.11), kind=kOutput, calls=%fused_computation.38 | output fusion | flops 50331648 | bytes 8651272 | tf_op jit(solution)/shard_map/jit(cumprod)/reduce_window | solution.py:44
  54.5 4.5 %slice.100 = f32[31,256,128]{2,1,0:T(8,128)} slice(f32[32,256,128]{2,1,0:T(8,128)} %fusion.22), slice={[0:31], [0:256], [0:128]} | slice | bytes 8126464 | tf_op jit(solution)/shard_map/slice | solution.py:45
  59.0 13.6 %add_multiply_fusion = (f32[32,256,128]{2,1,0:T(8,128)S(1)}, f32[32,256,128]{2,1,0:T(8,128)S(1)}) fusion(f32[34,258,130]{2,1,0:T(8,128)S(1)} %fusion.11, f32[31,256,128]{2,1,0:T(8,128)} %slice.100, f32[]{:T(128)} %bitcast.4, f32[]{:T(128)} %bitcast.3, pred[256]{0:T(512)(128)(4,1)S(1)} %gt.22, s32[256,128]{1,0:T(8,128)S(1)} %bitcast.42, ...), kind=kLoop, calls=%fused_computation.37 | loop fusion | flops 40894464 | bytes 42074376 | tf_op jit(solution)/shard_map/mul | solution.py:46
  72.6 3.8 %multiply_reduce_fusion = f32[3,256,128]{2,1,0:T(8,128)S(1)} fusion(f32[3]{0:T(128)S(1)} %get-tuple-element.156, f32[32,256,128]{2,1,0:T(8,128)S(1)} %get-tuple-element.148, f32[3]{0:T(128)S(1)} %get-tuple-element.155, f32[32,256,128]{2,1,0:T(8,128)S(1)} %get-tuple-element.147), kind=kLoop, calls=%fused_computation.9 | loop fusion | flops 21921792 | bytes 8781848 | tf_op jit(solution)/shard_map/reduce_sum | solution.py:50
  76.5 1.1 copy.19
  77.7 17.1 %all-to-all-start = ((f32[1,4,256,128]{3,1,0,2:T(4,128)}), f32[1,4,256,128]{3,1,0,2:T(4,128)S(1)}, u32[]{:S(2)}, u32[]{:S(2)}) async-start(f32[1,4,256,128]{3,1,0,2:T(4,128)} %copy.19), calls=%async_computation | async-start | bytes 1048576 | tf_op jit(solution)/shard_map/all_to_all | solution.py:76
  94.8 29.3 %all-to-all-done = f32[1,4,256,128]{3,1,0,2:T(4,128)S(1)} async-done(((f32[1,4,256,128]{3,1,0,2:T(4,128)}), f32[1,4,256,128]{3,1,0,2:T(4,128)S(1)}, u32[]{:S(2)}, u32[]{:S(2)}) %all-to-all-start) | async-done | bytes 524320 | tf_op jit(solution)/shard_map/all_to_all | solution.py:76
  124.1 41.5 %while.16 = (s32[]{:T(128)}, f32[3,16,128]{2,1,0:T(8,128)S(1)}, f32[16,128]{1,0:T(8,128)S(1)}, s32[16]{0:T(128)S(1)}, f32[16,4,16,128]{3,2,0,1:T(8,128)S(1)}, /*index=5*/s32[]{:T(128)}, s32[]{:T(128)}, s32[]{:T(128)}) while((s32[]{:T(128)}, f32[3,16,128]{2,1,0:T(8,128)S(1)}, f32[16,128]{1,0:T(8,128)S(1)}, s32[16]{0:T(128)S(1)}, ...), condition=%wide.region_3.4_spmd.clone, body=%wide.region_2.3_spmd.clone.sunk | while | flops 22534 | bytes 180378 | solution.py:66
  165.7 33.5 %all_gather.3 = f32[4,256,128]{2,1,0:T(8,128)S(1)} all-gather(f32[4,16,128]{2,1,0:T(8,128)S(1)} %pad_maximum_fusion), channel_id=1, replica_groups=mesh['tx'=4,'ty'=8,'depth'=16] {'depth'}, dimensions={1}, use_global_device_ids=true | all-gather | bytes 557056 | tf_op jit(solution)/shard_map/all_gather | solution.py:78
  (93 shorter events, 11.5 us)
Async XLA Ops:
  0.9 28.3 %collective-permute-start.1 = (bf16[32,1,128]{2,1,0:T(2,128)(2,1)S(1)}, bf16[32,1,128]{2,1,0:T(2,128)(2,1)S(1)}, u32[]{:S(2)}, u32[]{:S(2)}) collective-permute-start(bf16[32,1,128]{2,1,0:T(2,128)(2,1)S(1)} %get-tuple-element.153), channel_id=1, source_target_pairs={{0,16},{16,32},{32,48},{48,64},{64,80},{80,96},{96,112},{1,17},{17... | collective-permute-start | bytes 24584 | tf_op jit(solution)/shard_map/ppermute | solution.py:15
  2.7 26.5 %collective-permute-start.4 = (bf16[32,1,128]{2,1,0:T(2,128)(2,1)S(1)}, bf16[32,1,128]{2,1,0:T(2,128)(2,1)S(1)}, u32[]{:S(2)}, u32[]{:S(2)}) collective-permute-start(bf16[32,1,128]{2,1,0:T(2,128)(2,1)S(1)} %get-tuple-element.154), channel_id=1, source_target_pairs={{16,0},{32,16},{48,32},{64,48},{80,64},{96,80},{112,96},{17,1},{33... | collective-permute-start | bytes 24584 | tf_op jit(solution)/shard_map/ppermute | solution.py:16
  4.8 24.3 %collective-permute-start = (bf16[1,256,128]{2,1,0:T(8,128)(2,1)S(1)}, bf16[1,256,128]{2,1,0:T(8,128)(2,1)S(1)}, u32[]{:S(2)}, u32[]{:S(2)}) collective-permute-start(bf16[1,256,128]{2,1,0:T(8,128)(2,1)S(1)} %get-tuple-element.151), channel_id=1, source_target_pairs={{0,1},{1,2},{2,3},{3,4},{4,5},{5,6},{6,7},{7,8},{8,9},{9,10},{10,1... | collective-permute-start | bytes 196616 | tf_op jit(solution)/shard_map/ppermute | solution.py:15
  8.7 9.0 %copy-start.2 = (f32[4,2]{0,1:T(2,128)S(1)}, f32[4,2]{0,1:T(2,128)}, u32[]{:S(2)}) copy-start(f32[4,2]{0,1:T(2,128)} %param.9) | copy-start | bytes 100
  8.7 9.0 %copy-start.3 = (s32[1,32,1]{1,2,0:T(1,128)S(1)}, s32[1,32,1]{1,2,0:T(1,128)}, u32[]{:S(2)}) copy-start(s32[1,32,1]{1,2,0:T(1,128)} %param.12) | copy-start | bytes 388
  8.7 20.5 %collective-permute-start.5 = (bf16[1,256,128]{2,1,0:T(8,128)(2,1)S(1)}, bf16[1,256,128]{2,1,0:T(8,128)(2,1)S(1)}, u32[]{:S(2)}, u32[]{:S(2)}) collective-permute-start(bf16[1,256,128]{2,1,0:T(8,128)(2,1)S(1)} %get-tuple-element.152), channel_id=1, source_target_pairs={{1,0},{2,1},{3,2},{4,3},{5,4},{6,5},{7,6},{8,7},{9,8},{10,9},{11,1... | collective-permute-start | bytes 196616 | tf_op jit(solution)/shard_map/ppermute | solution.py:16
  16.3 5.6 %collective-permute-start.2 = (bf16[32,256,1]{1,0,2:T(8,128)(2,1)S(1)}, bf16[32,256,1]{1,0,2:T(8,128)(2,1)S(1)}, u32[]{:S(2)}, u32[]{:S(2)}) collective-permute-start(bf16[32,256,1]{1,0,2:T(8,128)(2,1)S(1)} %copy.23), channel_id=1, source_target_pairs={{0,128},{128,256},{256,384},{1,129},{129,257},{257,385},{2,130},{1... | collective-permute-start | bytes 49160 | tf_op jit(solution)/shard_map/ppermute | solution.py:15
  22.0 5.4 %collective-permute-start.3 = (bf16[32,256,1]{1,0,2:T(8,128)(2,1)S(1)}, bf16[32,256,1]{1,0,2:T(8,128)(2,1)S(1)}, u32[]{:S(2)}, u32[]{:S(2)}) collective-permute-start(bf16[32,256,1]{1,0,2:T(8,128)(2,1)S(1)} %copy.24), channel_id=1, source_target_pairs={{128,0},{256,128},{384,256},{129,1},{257,129},{385,257},{130,2},{2... | collective-permute-start | bytes 49160 | tf_op jit(solution)/shard_map/ppermute | solution.py:16
  29.2 17.7 %copy-start = (s32[1,256,128]{2,1,0:T(8,128)S(1)}, s32[1,256,128]{2,1,0:T(8,128)}, u32[]{:S(2)}) copy-start(s32[1,256,128]{2,1,0:T(8,128)} %param.11) | copy-start | bytes 393220
  29.2 17.7 %copy-start.1 = (s32[1,256,128]{2,1,0:T(8,128)S(1)}, s32[1,256,128]{2,1,0:T(8,128)}, u32[]{:S(2)}) copy-start(s32[1,256,128]{2,1,0:T(8,128)} %param.10) | copy-start | bytes 393220
  72.6 3.8 %slice-start = ((f32[32,256,128]{2,1,0:T(8,128)}), f32[1,256,128]{2,1,0:T(8,128)S(1)}, s32[]{:S(2)}) async-start(f32[32,256,128]{2,1,0:T(8,128)} %fusion.22), calls=%async_computation.1 | async-start | bytes 262144 | tf_op jit(solution)/shard_map/slice | solution.py:51
  76.5 47.7 %copy-start.4 = (s32[16]{0:T(128)S(1)}, s32[16]{0:T(128)}, u32[]{:S(2)}) copy-start(s32[16]{0:T(128)} %param.13) | copy-start | bytes 196
  77.7 46.4 %all-to-all-start = ((f32[1,4,256,128]{3,1,0,2:T(4,128)}), f32[1,4,256,128]{3,1,0,2:T(4,128)S(1)}, u32[]{:S(2)}, u32[]{:S(2)}) async-start(f32[1,4,256,128]{3,1,0,2:T(4,128)} %copy.19), calls=%async_computation | async-start | bytes 1048576 | tf_op jit(solution)/shard_map/all_to_all | solution.py:76
where the time goes:
time: 201 us; the launch traced here: 200 us
  other arithmetic  43 us (21%)
  blocking collectives  33.5 us (17%)
  waiting for transfers between devices  32.7 us (16%)
  loops' own time  31.7 us (16%)
  local copies, waits for them, and re-layouts  29.6 us (15%)
  starting transfers between devices  29.2 us (15%)
    all_gather x1, blocking collectives, shards(): return lax.all_gather(picture, 'depth', axis=1, tiled=True)  33.5 us
    another operation x1, loops' own time, composite(): colors, remain = lax.fori_loop(0, count, step, start_pair)  31.7 us
    all_to_all x1, waiting for transfers between devices, shards(): lax.all_to_all(stacked, 'depth', split_axis=2, concat_axis=0, tiled=True)  29.3 us
    convert_element_type x1, other arithmetic, shards(): extended(volume, (('tx', 2), ('ty', 1), ('depth', 0)), 1)  17.7 us
    all_to_all x1, starting transfers between devices, shards(): lax.all_to_all(stacked, 'depth', split_axis=2, concat_axis=0, tiled=True)  17.1 us
    mul x1, other arithmetic, local_partial(): weights = prior * opacity * shading  13.6 us
    dynamic_slice x16, local copies, waits for them, and re-layouts, step(): depth_order[position]  9.38 us
    another operation x1, other arithmetic, local_partial(): passed = jnp.cumprod(1.0 - opacity, axis=0)  7.63 us
  transfers between devices with their start and end apart: 7, of which 2 were waited for; matrix products, arithmetic and copies ran while one was open for 6% of the time, Pallas kernels for 0%

commit v1 on v0

v1 whole, which is shorter than its diff:
```python
import jax
import jax.numpy as jnp
from jax import lax
from jax.experimental import pallas as pl
from jax.experimental.pallas import tpu as pltpu
from jax.sharding import PartitionSpec as P

LOG2E = 1.4426950408889634
CODE = 65535.0
VMEM = pltpu.VMEM
SMEM = pltpu.SMEM


def iota(shape, dim):
    return lax.broadcasted_iota(jnp.int32, shape, dim)


def encode(low, high):
    def code(x):
        root = jnp.sqrt(jnp.sqrt(jnp.maximum(x, 0.0)))
        return jnp.minimum(root * CODE + 0.5, CODE).astype(jnp.int32)

    return code(low) | (code(high) << 16)


def decode(word):
    def value(c):
        square = (c.astype(jnp.float32) * (1.0 / CODE)) ** 2
        return square * square

    return value(word & 0xFFFF), value(lax.shift_right_logical(word, 16))


def edges_kernel(vol, z0, z1, y0, y1, xt):
    layers, rows, cols = vol.shape
    z0[...] = vol[0]
    z1[...] = vol[layers - 1]
    y0[...] = vol[:, 0:16, :][:, 0, :]
    y1[...] = vol[:, rows - 16 : rows, :][:, 15, :]
    r, c = (iota((2 * cols, cols), 0), iota((2 * cols, cols), 1))
    total = jnp.zeros((rows, cols), jnp.float32)
    for k in range(0, layers, 2):
        pick = ((r % cols == 0) & (c - r // cols == k)) | (
            (r % cols == cols - 1) & (c - r // cols == k + layers)
        )
        pair = jnp.concatenate([vol[k], vol[k + 1]], axis=1)
        total = total + jnp.dot(
            pair, pick.astype(jnp.float32).astype(jnp.bfloat16), preferred_element_type=jnp.float32
        )
    xt[...] = total.astype(jnp.bfloat16)


def render_kernel(
    tf, pat, vol, zlo, zhi, ylo, yhi, xlo, xhi, start, stop, out, sx_all, sy_all, count, step_rows
):
    layers, rows, cols = vol.shape
    f32, bf16 = (jnp.float32, jnp.bfloat16)

    lane = iota((rows, cols), 1)
    side = jnp.where(lane < layers, xhi[...].astype(f32), xlo[...].astype(f32)).astype(bf16)
    r, c = (iota((cols, cols), 0), iota((cols, cols), 1))
    dx = ((r == c + 1).astype(f32) - (r == c - 1).astype(f32)).astype(bf16)
    yr, yc = (iota((rows, rows), 0), iota((rows, rows), 1))
    dy = ((yc == yr + 1).astype(f32) - (yc == yr - 1).astype(f32)).astype(bf16)
    at_low, at_high = (jnp.where(c == 0, r, -1), jnp.where(c == cols - 1, r, -1))

    def gradients(k, carry):
        v = vol[k]
        ends = ((at_high == k).astype(f32) - (at_low == k + layers).astype(f32)).astype(bf16)
        sx_all[k] = jnp.dot(
            jnp.concatenate([v, side], axis=1),
            jnp.concatenate([dx, ends], axis=0),
            preferred_element_type=f32,
        )
        sy_all[k] = jnp.dot(dy, v, preferred_element_type=f32)
        return carry

    lax.fori_loop(0, layers, gradients, 0, unroll=2)
    sub = iota((layers, 8, cols), 1)
    sy_all[:, 0:8, :] = sy_all[:, 0:8, :] - jnp.where(sub == 0, ylo[...].astype(f32)[:, None, :], 0.0)
    sy_all[:, rows - 8 : rows, :] = sy_all[:, rows - 8 : rows, :] + jnp.where(
        sub == 7, yhi[...].astype(f32)[:, None, :], 0.0
    )

    slopes = [tf[j, 0] * 0.5 for j in range(3)]
    offsets = [tf[j, 1] * 0.5 for j in range(3)]
    dens_slope, dens_offset = (tf[3, 0] * LOG2E, tf[3, 1] * LOG2E)
    scale = -LOG2E * 2.0 / (layers * count)

    def chunk(i, carry):
        base = pl.multiple_of(i * step_rows, step_rows)
        here = pl.ds(base, step_rows)
        group = iota((step_rows, cols), 0) // 8
        begin, end = (start[here, :], stop[here, :])
        on = jnp.zeros((step_rows, cols), jnp.int32)
        for g in range(step_rows // 8):
            on = jnp.where(group == g, pat[i * (step_rows // 8) + g], on)
        end = jnp.where(on > 0, end, 0)
        zero = jnp.zeros((step_rows, cols), f32)
        depth, before, shaded = (zero, zero + 1.0, zero)
        tints = [zero, zero, zero]
        below, value = (zlo[here, :].astype(f32), vol[0, here, :].astype(f32))
        for k in range(layers):
            above = (vol[k + 1, here, :] if k + 1 < layers else zhi[here, :]).astype(f32)
            sx, sy, sz = (sx_all[k, here, :], sy_all[k, here, :], above - below)
            lit = jnp.abs((0.48 * 0.7) * sx + (0.6 * 0.7) * sy + (0.64 * 0.7) * sz)
            shading = 0.3 + lit * lax.rsqrt(sx * sx + sy * sy + sz * sz + 4.0)
            soft = jnp.log(1.0 + jnp.exp2(dens_slope * value + dens_offset))
            active = (begin <= k) & (end > k)
            depth = depth + jnp.where(active, soft, 0.0)
            after = jnp.exp2(depth * scale)
            weight = (before - after) * shading
            shaded = shaded + weight
            tints = [
                t + weight * jnp.tanh(s * value + o) for t, s, o in zip(tints, slopes, offsets)
            ]
            below, value, before = (value, above, after)
        red, green, blue = [0.5 * (shaded + t) for t in tints]
        first, second = (encode(red, green), encode(blue, 1.0 - before))
        share = rows // count
        for j in range(step_rows // share):
            out[i * (step_rows // share) + j, 0] = first[j * share : (j + 1) * share]
            out[i * (step_rows // share) + j, 1] = second[j * share : (j + 1) * share]
        return carry

    lax.fori_loop(0, rows // step_rows, chunk, 0)


def composite_kernel(order, parts, out):
    count, _, rows, cols = parts.shape

    def step(r, state):
        red, green, blue, left = state
        s = order[r]
        one, two = (decode(parts[s, 0]), decode(parts[s, 1]))
        return (red + left * one[0], green + left * one[1], blue + left * two[0], left * (1.0 - two[1]))

    zero = jnp.zeros((rows, cols), jnp.float32)
    state = (zero, zero, zero, zero + 1.0)
    for r in range(count):
        state = step(r, state)
    red, green, blue, left = state
    first, second = (encode(red, green), encode(blue, 1.0 - left))
    for s in range(count):
        out[s, 0] = first
        out[s, 1] = second


def frame_kernel(words, out):
    count, _, rows, cols = words.shape
    for s in range(count):
        here = slice(s * rows, (s + 1) * rows)
        for w in range(2):
            low, high = decode(words[s, w])
            out[2 * w, here, :] = low
            out[2 * w + 1, here, :] = high


def halo(array, axis, shift):
    count = lax.axis_size(axis)
    pairs = [(i, i + shift) for i in range(count) if 0 <= i + shift < count]
    return lax.ppermute(array, axis, pairs)


def shards(volume, transfer, ray_start, ray_stop, pattern, depth_order):
    layers, rows, cols = volume.shape
    count = lax.axis_size("depth")
    bf16, f32 = (jnp.bfloat16, jnp.float32)
    limit = pltpu.CompilerParams(vmem_limit_bytes=40 * 1024 * 1024)
    vmem = pl.BlockSpec(memory_space=VMEM)
    smem = pl.BlockSpec(memory_space=SMEM)
    shape = jax.ShapeDtypeStruct

    z0, z1, y0, y1, xt = pl.pallas_call(
        edges_kernel,
        out_shape=[
            shape((rows, cols), bf16),
            shape((rows, cols), bf16),
            shape((layers, cols), bf16),
            shape((layers, cols), bf16),
            shape((rows, cols), bf16),
        ],
        in_specs=[vmem],
        out_specs=[vmem] * 5,
        compiler_params=limit,
        name="edges",
    )(volume)
    zlo, zhi = (halo(z1, "depth", 1), halo(z0, "depth", -1))
    ylo, yhi = (halo(y1, "ty", 1), halo(y0, "ty", -1))
    xlo, xhi = (halo(xt, "tx", 1), halo(xt, "tx", -1))

    step_rows = 32
    share = rows // count
    words = pl.pallas_call(
        lambda *refs: render_kernel(*refs, count=count, step_rows=step_rows),
        out_shape=shape((count, 2, share, cols), jnp.int32),
        in_specs=[smem, smem] + [vmem] * 9,
        out_specs=vmem,
        scratch_shapes=[VMEM((layers, rows, cols), f32), VMEM((layers, rows, cols), f32)],
        compiler_params=limit,
        name="render",
    )(transfer, pattern.reshape(-1), volume, zlo, zhi, ylo, yhi, xlo, xhi, ray_start[0], ray_stop[0])

    words = lax.all_to_all(words, "depth", split_axis=0, concat_axis=0, tiled=True)
    words = pl.pallas_call(
        composite_kernel,
        out_shape=shape(words.shape, jnp.int32),
        in_specs=[smem, vmem],
        out_specs=vmem,
        compiler_params=limit,
        name="composite",
    )(depth_order, words)
    words = lax.all_to_all(words, "depth", split_axis=0, concat_axis=0, tiled=True)
    return pl.pallas_call(
        frame_kernel,
        out_shape=shape((4, rows, cols), f32),
        in_specs=[vmem],
        out_specs=vmem,
        compiler_params=limit,
        name="frame",
    )(words)


def solution(mesh):
    in_specs = (
        P("depth", "ty", "tx"),
        P(),
        P("depth", "ty", "tx"),
        P("depth", "ty", "tx"),
        P("depth", "ty", "tx"),
        P(),
    )
    out_specs = P(None, "ty", "tx")
    return jax.shard_map(shards, mesh=mesh, in_specs=in_specs, out_specs=out_specs, check_vma=False)
```

time: 201 us -> 98.7 us (0.49)
  the two profiles are of different devices: /device:TPU:24 before, /device:TPU:6 now
where the time goes in v1:
time: 98.7 us; the launch traced here: 96.9 us
  blocking collectives  59.4 us (60%)
  Pallas kernels  14.8 us (15%)
  starting transfers between devices  14.8 us (15%)
  waiting for transfers between devices  4.29 us (4%)
  local copies, waits for them, and re-layouts  3.5 us (4%)
    all_to_all x2, blocking collectives, shards(): lax.all_to_all(words, 'depth', split_axis=0, concat_axis=0, tiled=True)  59.4 us
    ppermute x6, starting transfers between devices, halo(): return lax.ppermute(array, axis, pairs)  14.8 us
    pallas_call x1, Pallas kernels, shards(): pl.pallas_call(lambda *refs: render_kernel(*refs, count=count, step_rows=...  12.5 us
    ppermute x6, waiting for transfers between devices, halo(): return lax.ppermute(array, axis, pairs)  4.29 us
    unnamed x15, local copies, waits for them, and re-layouts  3.5 us
  transfers between devices with their start and end apart: 6, of which 2 were waited for; matrix products, arithmetic and copies ran while one was open for 0% of the time, Pallas kernels for 0%

profile of v1, /device:TPU:6, one launch (start us, length us, event | category | flops | bytes accessed | tf_op | source)
XLA Modules:
  0.0 96.9 jit_solution(7391395163573375428)
XLA Ops:
  0.0 1.6 %copy-done = bf16[32,256,128]{2,1,0:T(8,128)(2,1)S(1)} copy-done((bf16[32,256,128]{2,1,0:T(8,128)(2,1)S(1)}, bf16[32,256,128]{2,1,0:T(8,128)(2,1)}, u32[]{:S(2)}) %copy-start) | copy-done | bytes 2097176
  1.6 0.7 edges.1
  2.3 0.0 copy-start.4
  2.3 3.8 %collective-permute-start = (bf16[256,128]{1,0:T(8,128)(2,1)S(1)}, bf16[256,128]{1,0:T(8,128)(2,1)S(1)}, u32[]{:S(2)}, u32[]{:S(2)}) collective-permute-start(bf16[256,128]{1,0:T(8,128)(2,1)S(1)} %get-tuple-element.10), channel_id=1, source_target_pairs={{0,1},{1,2},{2,3},{3,4},{4,5},{5,6},{6,7},{7,8},{8,9},{9,10},{10,1... | collective-permute-start | bytes 196616 | tf_op jit(solution)/shard_map/ppermute | solution.py:162
  6.2 1.3 %collective-permute-start.1 = (bf16[256,128]{1,0:T(8,128)(2,1)S(1)}, bf16[256,128]{1,0:T(8,128)(2,1)S(1)}, u32[]{:S(2)}, u32[]{:S(2)}) collective-permute-start(bf16[256,128]{1,0:T(8,128)(2,1)S(1)} %get-tuple-element.11), channel_id=1, source_target_pairs={{1,0},{2,1},{3,2},{4,3},{5,4},{6,5},{7,6},{8,7},{9,8},{10,9},{11,1... | collective-permute-start | bytes 196616 | tf_op jit(solution)/shard_map/ppermute | solution.py:162
  7.5 1.3 %collective-permute-start.5 = (bf16[256,128]{1,0:T(8,128)(2,1)S(1)}, bf16[256,128]{1,0:T(8,128)(2,1)S(1)}, u32[]{:S(2)}, u32[]{:S(2)}) collective-permute-start(bf16[256,128]{1,0:T(8,128)(2,1)S(1)} %get-tuple-element.14), channel_id=1, source_target_pairs={{128,0},{256,128},{384,256},{129,1},{257,129},{385,257},{130,2},{2... | collective-permute-start | bytes 196616 | tf_op jit(solution)/shard_map/ppermute | solution.py:162
  8.8 4.5 %collective-permute-start.4 = (bf16[256,128]{1,0:T(8,128)(2,1)S(1)}, bf16[256,128]{1,0:T(8,128)(2,1)S(1)}, u32[]{:S(2)}, u32[]{:S(2)}) collective-permute-start(bf16[256,128]{1,0:T(8,128)(2,1)S(1)} %get-tuple-element.14), channel_id=1, source_target_pairs={{0,128},{128,256},{256,384},{1,129},{129,257},{257,385},{2,130},{1... | collective-permute-start | bytes 196616 | tf_op jit(solution)/shard_map/ppermute | solution.py:162
  13.3 1.9 %collective-permute-start.2 = (bf16[32,128]{1,0:T(8,128)(2,1)S(1)}, bf16[32,128]{1,0:T(8,128)(2,1)S(1)}, u32[]{:S(2)}, u32[]{:S(2)}) collective-permute-start(bf16[32,128]{1,0:T(8,128)(2,1)S(1)} %get-tuple-element.12), channel_id=1, source_target_pairs={{0,16},{16,32},{32,48},{48,64},{64,80},{80,96},{96,112},{1,17},{17... | collective-permute-start | bytes 24584 | tf_op jit(solution)/shard_map/ppermute | solution.py:162
  15.3 3.0 %collective-permute-done.2.refs_5_ = bf16[32,128]{1,0:T(8,128)(2,1)S(1)} collective-permute-done((bf16[32,128]{1,0:T(8,128)(2,1)S(1)}, bf16[32,128]{1,0:T(8,128)(2,1)S(1)}, u32[]{:S(2)}, u32[]{:S(2)}) %collective-permute-start.2) | collective-permute-done | bytes 8224 | tf_op jit(solution)/shard_map/ppermute | solution.py:162
  18.3 1.9 %collective-permute-start.3 = (bf16[32,128]{1,0:T(8,128)(2,1)S(1)}, bf16[32,128]{1,0:T(8,128)(2,1)S(1)}, u32[]{:S(2)}, u32[]{:S(2)}) collective-permute-start(bf16[32,128]{1,0:T(8,128)(2,1)S(1)} %get-tuple-element.13), channel_id=1, source_target_pairs={{16,0},{32,16},{48,32},{64,48},{80,64},{96,80},{112,96},{17,1},{33... | collective-permute-start | bytes 24584 | tf_op jit(solution)/shard_map/ppermute | solution.py:162
  20.2 0.1 copy.7.refs_0_
  20.3 1.2 %collective-permute-done.3.refs_6_ = bf16[32,128]{1,0:T(8,128)(2,1)S(1)} collective-permute-done((bf16[32,128]{1,0:T(8,128)(2,1)S(1)}, bf16[32,128]{1,0:T(8,128)(2,1)S(1)}, u32[]{:S(2)}, u32[]{:S(2)}) %collective-permute-start.3) | collective-permute-done | bytes 8224 | tf_op jit(solution)/shard_map/ppermute | solution.py:162
  21.6 0.0 collective-permute-done.refs_3_
  21.6 0.0 collective-permute-done.1.refs_4_
  21.6 0.0 collective-permute-done.5.refs_8_
  21.6 0.0 collective-permute-done.4.refs_7_
  21.6 0.0 copy-start.2
  21.6 0.9 copy-done.2
  22.5 0.9 copy-done.3
  23.4 12.5 %render.1 = s32[16,2,16,128]{3,2,1,0:T(8,128)S(1)} custom-call(f32[4,2]{1,0:T(4,128)S(1)} %copy.7.refs_0_, s32[32]{0:T(128)S(1)} %bitcast.5, bf16[32,256,128]{2,1,0:T(8,128)(2,1)S(1)} %copy-done.1, bf16[256,128]{1,0:T(8,128)(2,1)S(1)} %collective-permute-done.refs_3_, bf16[256,128]{1,0:T(8,128)(2,1)S(1)} %collective-permute-done.1.refs_4_, ...), custom_call_target="tpu_custom_call" | custom-call | tf_op jit(solution)/shard_map/render/pallas_call | solution.py:194
  35.9 35.3 %all_to_all.10.parts = s32[16,2,16,128]{3,2,1,0:T(8,128)S(1)} all-to-all(s32[16,2,16,128]{3,2,1,0:T(8,128)S(1)} %render.1), channel_id=1, replica_groups=mesh['tx'=4,'ty'=8,'depth'=16] {'depth'}, dimensions={0} | all-to-all | bytes 524288 | tf_op jit(solution)/shard_map/all_to_all | solution.py:204
  71.2 0.7 composite.1
  71.9 24.1 %all_to_all.11.words = s32[16,2,16,128]{3,2,1,0:T(8,128)S(1)} all-to-all(s32[16,2,16,128]{3,2,1,0:T(8,128)S(1)} %composite.1), channel_id=1, replica_groups=mesh['tx'=4,'ty'=8,'depth'=16] {'depth'}, dimensions={0} | all-to-all | bytes 524288 | tf_op jit(solution)/shard_map/all_to_all | solution.py:213
  96.1 0.9 frame.1
  (9 shorter events, 0.0 us)
Async XLA Ops:
  0.0 1.6 %copy-start = (bf16[32,256,128]{2,1,0:T(8,128)(2,1)S(1)}, bf16[32,256,128]{2,1,0:T(8,128)(2,1)}, u32[]{:S(2)}) copy-start(bf16[32,256,128]{2,1,0:T(8,128)(2,1)} %refs_2_.1) | copy-start | bytes 6291460
  1.6 18.6 %copy-start.6 = (f32[4,2]{0,1:T(2,128)S(1)}, f32[4,2]{0,1:T(2,128)}, u32[]{:S(2)}) copy-start(f32[4,2]{0,1:T(2,128)} %param.7) | copy-start | bytes 100
  1.6 20.0 %copy-start.1 = (bf16[32,256,128]{2,1,0:T(8,128)(2,1)S(1)}, bf16[32,256,128]{2,1,0:T(8,128)(2,1)}, u32[]{:S(2)}) copy-start(bf16[32,256,128]{2,1,0:T(8,128)(2,1)} %refs_2_.1) | copy-start | bytes 6291460
  1.6 20.0 %copy-start.5 = (s32[1,32,1]{1,2,0:T(1,128)S(1)}, s32[1,32,1]{1,2,0:T(1,128)}, u32[]{:S(2)}) copy-start(s32[1,32,1]{1,2,0:T(1,128)} %param.10) | copy-start | bytes 388
  2.3 68.9 %copy-start.4 = (s32[16]{0:T(128)S(1)}, s32[16]{0:T(128)}, u32[]{:S(2)}) copy-start(s32[16]{0:T(128)} %order.1) | copy-start | bytes 196
  2.3 19.2 %collective-permute-start = (bf16[256,128]{1,0:T(8,128)(2,1)S(1)}, bf16[256,128]{1,0:T(8,128)(2,1)S(1)}, u32[]{:S(2)}, u32[]{:S(2)}) collective-permute-start(bf16[256,128]{1,0:T(8,128)(2,1)S(1)} %get-tuple-element.10), channel_id=1, source_target_pairs={{0,1},{1,2},{2,3},{3,4},{4,5},{5,6},{6,7},{7,8},{8,9},{9,10},{10,1... | collective-permute-start | bytes 196616 | tf_op jit(solution)/shard_map/ppermute | solution.py:162
  6.2 15.4 %collective-permute-start.1 = (bf16[256,128]{1,0:T(8,128)(2,1)S(1)}, bf16[256,128]{1,0:T(8,128)(2,1)S(1)}, u32[]{:S(2)}, u32[]{:S(2)}) collective-permute-start(bf16[256,128]{1,0:T(8,128)(2,1)S(1)} %get-tuple-element.11), channel_id=1, source_target_pairs={{1,0},{2,1},{3,2},{4,3},{5,4},{6,5},{7,6},{8,7},{9,8},{10,9},{11,1... | collective-permute-start | bytes 196616 | tf_op jit(solution)/shard_map/ppermute | solution.py:162
  7.5 14.1 %collective-permute-start.5 = (bf16[256,128]{1,0:T(8,128)(2,1)S(1)}, bf16[256,128]{1,0:T(8,128)(2,1)S(1)}, u32[]{:S(2)}, u32[]{:S(2)}) collective-permute-start(bf16[256,128]{1,0:T(8,128)(2,1)S(1)} %get-tuple-element.14), channel_id=1, source_target_pairs={{128,0},{256,128},{384,256},{129,1},{257,129},{385,257},{130,2},{2... | collective-permute-start | bytes 196616 | tf_op jit(solution)/shard_map/ppermute | solution.py:162
  8.8 12.8 %collective-permute-start.4 = (bf16[256,128]{1,0:T(8,128)(2,1)S(1)}, bf16[256,128]{1,0:T(8,128)(2,1)S(1)}, u32[]{:S(2)}, u32[]{:S(2)}) collective-permute-start(bf16[256,128]{1,0:T(8,128)(2,1)S(1)} %get-tuple-element.14), channel_id=1, source_target_pairs={{0,128},{128,256},{256,384},{1,129},{129,257},{257,385},{2,130},{1... | collective-permute-start | bytes 196616 | tf_op jit(solution)/shard_map/ppermute | solution.py:162
  13.3 5.0 %collective-permute-start.2 = (bf16[32,128]{1,0:T(8,128)(2,1)S(1)}, bf16[32,128]{1,0:T(8,128)(2,1)S(1)}, u32[]{:S(2)}, u32[]{:S(2)}) collective-permute-start(bf16[32,128]{1,0:T(8,128)(2,1)S(1)} %get-tuple-element.12), channel_id=1, source_target_pairs={{0,16},{16,32},{32,48},{48,64},{64,80},{80,96},{96,112},{1,17},{17... | collective-permute-start | bytes 24584 | tf_op jit(solution)/shard_map/ppermute | solution.py:162
  18.3 3.3 %collective-permute-start.3 = (bf16[32,128]{1,0:T(8,128)(2,1)S(1)}, bf16[32,128]{1,0:T(8,128)(2,1)S(1)}, u32[]{:S(2)}, u32[]{:S(2)}) collective-permute-start(bf16[32,128]{1,0:T(8,128)(2,1)S(1)} %get-tuple-element.13), channel_id=1, source_target_pairs={{16,0},{32,16},{48,32},{64,48},{80,64},{96,80},{112,96},{17,1},{33... | collective-permute-start | bytes 24584 | tf_op jit(solution)/shard_map/ppermute | solution.py:162
  21.6 0.9 copy-start.2
  22.5 0.9 copy-start.3

commit v2 on v1

v2 whole, which is shorter than its diff:
```python
import jax
import jax.numpy as jnp
from jax import lax
from jax.experimental import pallas as pl
from jax.experimental.pallas import tpu as pltpu
from jax.sharding import PartitionSpec as P

LOG2E = 1.4426950408889634
CODE = 65535.0
VMEM = pltpu.VMEM
SMEM = pltpu.SMEM


def iota(shape, dim):
    return lax.broadcasted_iota(jnp.int32, shape, dim)


def encode(low, high):
    def code(x):
        root = jnp.sqrt(jnp.sqrt(jnp.maximum(x, 0.0)))
        return jnp.minimum(root * CODE + 0.5, CODE).astype(jnp.int32)

    return code(low) | (code(high) << 16)


def decode(word):
    def value(c):
        square = (c.astype(jnp.float32) * (1.0 / CODE)) ** 2
        return square * square

    return value(word & 0xFFFF), value(lax.shift_right_logical(word, 16))


def faces_kernel(vol, z0, z1, y0, y1, first, last, sems):
    layers, rows, _ = vol.shape
    copies = [
        pltpu.make_async_copy(vol.at[0], z0, sems.at[0]),
        pltpu.make_async_copy(vol.at[layers - 1], z1, sems.at[1]),
        pltpu.make_async_copy(vol.at[:, pl.ds(0, 16), :], first, sems.at[2]),
        pltpu.make_async_copy(vol.at[:, pl.ds(rows - 16, 16), :], last, sems.at[3]),
    ]
    for copy in copies:
        copy.start()
    for copy in copies:
        copy.wait()
    y0[...] = first[...][:, 0, :]
    y1[...] = last[...][:, 15, :]


def sides_kernel(vol, arrived, xt):
    layers, rows, cols = vol.shape
    r, c = (iota((2 * cols, cols), 0), iota((2 * cols, cols), 1))
    total = jnp.zeros((rows, cols), jnp.float32)
    for k in range(0, layers, 2):
        pick = ((r % cols == 0) & (c - r // cols == k)) | (
            (r % cols == cols - 1) & (c - r // cols == k + layers)
        )
        pair = jnp.concatenate([vol[k], vol[k + 1]], axis=1)
        total = total + jnp.dot(
            pair, pick.astype(jnp.float32).astype(jnp.bfloat16), preferred_element_type=jnp.float32
        )
    xt[...] = total.astype(jnp.bfloat16)


def absorb_kernel(tf, pat, vol, start, stop, weights, alpha, begin, end, sems, count, step_rows):
    layers, rows, cols = vol.shape
    f32 = jnp.float32
    copies = [
        pltpu.make_async_copy(start, begin, sems.at[0]),
        pltpu.make_async_copy(stop, end, sems.at[1]),
    ]
    for copy in copies:
        copy.start()
    for copy in copies:
        copy.wait()
    slope, offset = (tf[3, 0] * LOG2E, tf[3, 1] * LOG2E)
    scale = -LOG2E * 2.0 / (layers * count)
    half = layers // 2

    def chunk(i, carry):
        here = pl.ds(pl.multiple_of(i * step_rows, step_rows), step_rows)
        group = iota((step_rows, cols), 0) // 8
        on = jnp.zeros((step_rows, cols), jnp.int32)
        for g in range(step_rows // 8):
            on = jnp.where(group == g, pat[i * (step_rows // 8) + g], on)
        enter = jnp.where(on > 0, begin[here, :], layers)
        leave = jnp.where(on > 0, end[here, :], 0)
        depth = jnp.zeros((step_rows, cols), f32)
        before = depth + 1.0
        for k in range(layers):
            soft = jnp.log(1.0 + jnp.exp2(slope * vol[k, here, :].astype(f32) + offset))
            active = enter <= k if k < half else leave > k
            depth = depth + jnp.where(active, soft, 0.0)
            after = jnp.exp2(depth * scale)
            weights[k, here, :] = before - after
            before = after
        alpha[here, :] = 1.0 - before
        return carry

    lax.fori_loop(0, rows // step_rows, chunk, 0)


def shade_kernel(
    tf, vol, weights, alpha, zlo, zhi, ylo, yhi, xlo, xhi, out, field, sx_all, count, step_rows
):
    layers, rows, cols = vol.shape
    f32, bf16 = (jnp.float32, jnp.bfloat16)
    lane = iota((rows, cols), 1)
    side = jnp.where(lane < layers, xhi[...].astype(f32), xlo[...].astype(f32))
    r, c = (iota((2 * cols, cols), 0), iota((2 * cols, cols), 1))
    inner = r < cols
    plus = ((r == c + 1) & inner) | ((r >= cols) & (r < cols + layers) & (c == cols - 1))
    minus = ((r == c - 1) & inner) | ((r >= cols + layers) & (r < cols + 2 * layers) & (c == 0))
    delta = (plus.astype(f32) - minus.astype(f32)).astype(bf16)
    phase = jnp.where(lane < 2 * layers, lane % layers, layers)

    sub = iota((layers, 8, cols), 1)
    field[:, 0:8, :] = jnp.where(sub == 7, ylo[...].astype(f32)[:, None, :], 0.0)
    field[:, rows + 8 : rows + 16, :] = jnp.where(sub == 0, yhi[...].astype(f32)[:, None, :], 0.0)

    def along_x(k, carry):
        value = vol[k]
        field[k, 8 : rows + 8, :] = value.astype(f32)
        ends = jnp.where(phase == k, side, 0.0).astype(bf16)
        sx_all[k] = jnp.dot(
            jnp.concatenate([value, ends], axis=1), delta, preferred_element_type=f32
        )
        return carry

    lax.fori_loop(0, layers, along_x, 0, unroll=8)

    slopes = [tf[j, 0] * 0.5 for j in range(3)]
    offsets = [tf[j, 1] * 0.5 for j in range(3)]
    strength = 0.64 * 0.7

    def chunk(i, carry):
        base = pl.multiple_of(i * step_rows, step_rows)
        here = pl.ds(base, step_rows)
        zero = jnp.zeros((step_rows, cols), f32)
        shaded, tints = (zero, [zero, zero, zero])
        middle = pl.ds(pl.multiple_of(base + 8, 8), step_rows)
        below, value = (zlo[here, :].astype(f32), field[0, middle, :])
        for k in range(layers):
            above = field[k + 1, middle, :] if k + 1 < layers else zhi[here, :].astype(f32)
            sx, sz = (sx_all[k, here, :], above - below)
            sy = field[k, pl.ds(base + 9, step_rows), :] - field[k, pl.ds(base + 7, step_rows), :]
            lit = jnp.abs((0.48 / 0.64) * sx + (0.6 / 0.64) * sy + sz)
            bright = lit * lax.rsqrt(sx * sx + sy * sy + sz * sz + 4.0) + 0.3 / strength
            weight = weights[k, here, :] * bright
            shaded = shaded + weight
            tints = [
                t + weight * jnp.tanh(s * value + o) for t, s, o in zip(tints, slopes, offsets)
            ]
            below, value = (value, above)
        red, green, blue = [(0.5 * strength) * (shaded + t) for t in tints]
        first, second = (encode(red, green), encode(blue, alpha[here, :]))
        share = rows // count
        for j in range(step_rows // share):
            out[i * (step_rows // share) + j, 0] = first[j * share : (j + 1) * share]
            out[i * (step_rows // share) + j, 1] = second[j * share : (j + 1) * share]
        return carry

    lax.fori_loop(0, rows // step_rows, chunk, 0)


def composite_kernel(order, parts, out):
    count, _, rows, cols = parts.shape

    def step(r, state):
        red, green, blue, left = state
        s = order[r]
        one, two = (decode(parts[s, 0]), decode(parts[s, 1]))
        return (red + left * one[0], green + left * one[1], blue + left * two[0], left * (1.0 - two[1]))

    zero = jnp.zeros((rows, cols), jnp.float32)
    state = (zero, zero, zero, zero + 1.0)
    for r in range(count):
        state = step(r, state)
    red, green, blue, left = state
    first, second = (encode(red, green), encode(blue, 1.0 - left))
    for s in range(count):
        out[s, 0] = first
        out[s, 1] = second


def frame_kernel(words, out):
    count, _, rows, cols = words.shape
    for s in range(count):
        here = slice(s * rows, (s + 1) * rows)
        for w in range(2):
            low, high = decode(words[s, w])
            out[2 * w, here, :] = low
            out[2 * w + 1, here, :] = high


def halo(array, axis, shift):
    count = lax.axis_size(axis)
    pairs = [(i, i + shift) for i in range(count) if 0 <= i + shift < count]
    return lax.ppermute(array, axis, pairs)


def shards(volume, transfer, ray_start, ray_stop, pattern, depth_order):
    layers, rows, cols = volume.shape
    count = lax.axis_size("depth")
    bf16, f32 = (jnp.bfloat16, jnp.float32)
    limit = pltpu.CompilerParams(vmem_limit_bytes=32 * 1024 * 1024)
    vmem = pl.BlockSpec(memory_space=VMEM)
    smem = pl.BlockSpec(memory_space=SMEM)
    shape = jax.ShapeDtypeStruct

    hbm = pl.BlockSpec(memory_space=pltpu.HBM)
    anywhere = pl.BlockSpec(memory_space=pl.ANY)

    z0, z1, y0, y1 = pl.pallas_call(
        faces_kernel,
        out_shape=[shape((rows, cols), bf16)] * 2 + [shape((layers, cols), bf16)] * 2,
        in_specs=[hbm],
        out_specs=[vmem] * 4,
        scratch_shapes=[VMEM((layers, 16, cols), bf16)] * 2 + [pltpu.SemaphoreType.DMA((4,))],
        compiler_params=limit,
        name="faces",
    )(volume)
    zlo, zhi = (halo(z1, "depth", 1), halo(z0, "depth", -1))
    ylo, yhi = (halo(y1, "ty", 1), halo(y0, "ty", -1))
    xt = pl.pallas_call(
        sides_kernel,
        out_shape=shape((rows, cols), bf16),
        in_specs=[vmem, anywhere],
        out_specs=vmem,
        compiler_params=limit,
        name="sides",
    )(volume, zlo)
    xlo, xhi = (halo(xt, "tx", 1), halo(xt, "tx", -1))

    step_rows = 32
    share = rows // count
    weights, alpha = pl.pallas_call(
        lambda *refs: absorb_kernel(*refs, count=count, step_rows=step_rows),
        out_shape=[shape((layers, rows, cols), f32), shape((rows, cols), f32)],
        in_specs=[smem, smem, vmem, hbm, hbm],
        out_specs=[vmem] * 2,
        scratch_shapes=[VMEM((rows, cols), jnp.int32)] * 2 + [pltpu.SemaphoreType.DMA((2,))],
        compiler_params=limit,
        cost_estimate=pl.CostEstimate(
            flops=12 * volume.size, bytes_accessed=6 * volume.size, transcendentals=3 * volume.size
        ),
        name="absorb",
    )(transfer, pattern.reshape(-1), volume, ray_start[0], ray_stop[0])
    words = pl.pallas_call(
        lambda *refs: shade_kernel(*refs, count=count, step_rows=step_rows),
        out_shape=shape((count, 2, share, cols), jnp.int32),
        in_specs=[smem] + [vmem] * 9,
        out_specs=vmem,
        scratch_shapes=[VMEM((layers, rows + 16, cols), f32), VMEM((layers, rows, cols), f32)],
        compiler_params=limit,
        cost_estimate=pl.CostEstimate(
            flops=40 * volume.size, bytes_accessed=6 * volume.size, transcendentals=4 * volume.size
        ),
        name="shade",
    )(transfer, volume, weights, alpha, zlo, zhi, ylo, yhi, xlo, xhi)

    words = lax.all_to_all(words, "depth", split_axis=0, concat_axis=0, tiled=True)
    words = pl.pallas_call(
        composite_kernel,
        out_shape=shape(words.shape, jnp.int32),
        in_specs=[smem, vmem],
        out_specs=vmem,
        compiler_params=limit,
        name="composite",
    )(depth_order, words)
    words = lax.all_to_all(words, "depth", split_axis=0, concat_axis=0, tiled=True)
    return pl.pallas_call(
        frame_kernel,
        out_shape=shape((4, rows, cols), f32),
        in_specs=[vmem],
        out_specs=vmem,
        compiler_params=limit,
        name="frame",
    )(words)


def solution(mesh):
    in_specs = (
        P("depth", "ty", "tx"),
        P(),
        P("depth", "ty", "tx"),
        P("depth", "ty", "tx"),
        P("depth", "ty", "tx"),
        P(),
    )
    out_specs = P(None, "ty", "tx")
    return jax.shard_map(shards, mesh=mesh, in_specs=in_specs, out_specs=out_specs, check_vma=False)
```

time: 98.7 us -> 91.4 us (0.926)
  the two profiles are of different devices: /device:TPU:6 before, /device:TPU:18 now
where the time goes in v2:
time: 91.4 us; the launch traced here: 91.1 us
  blocking collectives  59.1 us (65%)
  starting transfers between devices  16.7 us (18%)
  Pallas kernels  12.9 us (14%)
  local copies, waits for them, and re-layouts  1.71 us (2%)
    all_to_all x2, blocking collectives, shards(): lax.all_to_all(words, 'depth', split_axis=0, concat_axis=0, tiled=True)  59.1 us
    ppermute x6, starting transfers between devices, halo(): return lax.ppermute(array, axis, pairs)  16.7 us
    pallas_call x1, Pallas kernels, shards(): pl.pallas_call(lambda *refs: shade_kernel(*refs, count=count, step_rows=s...  7.46 us
    pallas_call x1, Pallas kernels, shards(): pl.pallas_call(lambda *refs: absorb_kernel(*refs, count=count, step_rows=...  2.83 us
  transfers between devices with their start and end apart: 6, of which 1 were waited for; matrix products, arithmetic and copies ran while one was open for 0% of the time, Pallas kernels for 4%

profile of v2, /device:TPU:18, one launch (start us, length us, event | category | flops | bytes accessed | tf_op | source)
XLA Modules:
  0.0 91.1 jit_solution(1574407614867385910)
XLA Ops:
  0.0 1.6 %copy-done = bf16[32,256,128]{2,1,0:T(8,128)(2,1)S(1)} copy-done((bf16[32,256,128]{2,1,0:T(8,128)(2,1)S(1)}, bf16[32,256,128]{2,1,0:T(8,128)(2,1)}, u32[]{:S(2)}) %copy-start) | copy-done | bytes 2097176
  1.6 0.3 faces.1
  1.9 4.0 %collective-permute-start = (bf16[256,128]{1,0:T(8,128)(2,1)S(1)}, bf16[256,128]{1,0:T(8,128)(2,1)S(1)}, u32[]{:S(2)}, u32[]{:S(2)}) collective-permute-start(bf16[256,128]{1,0:T(8,128)(2,1)S(1)} %get-tuple-element.13), channel_id=1, source_target_pairs={{0,1},{1,2},{2,3},{3,4},{4,5},{5,6},{6,7},{7,8},{8,9},{9,10},{10,1... | collective-permute-start | bytes 196616 | tf_op jit(solution)/shard_map/ppermute | solution.py:199
  5.9 1.3 %collective-permute-start.1 = (bf16[256,128]{1,0:T(8,128)(2,1)S(1)}, bf16[256,128]{1,0:T(8,128)(2,1)S(1)}, u32[]{:S(2)}, u32[]{:S(2)}) collective-permute-start(bf16[256,128]{1,0:T(8,128)(2,1)S(1)} %get-tuple-element.14), channel_id=1, source_target_pairs={{1,0},{2,1},{3,2},{4,3},{5,4},{6,5},{7,6},{8,7},{9,8},{10,9},{11,1... | collective-permute-start | bytes 196616 | tf_op jit(solution)/shard_map/ppermute | solution.py:199
  7.2 0.6 collective-permute-done.arrived.refs_4_
  7.7 0.7 sides.1
  8.5 2.4 %collective-permute-start.5 = (bf16[256,128]{1,0:T(8,128)(2,1)S(1)}, bf16[256,128]{1,0:T(8,128)(2,1)S(1)}, u32[]{:S(2)}, u32[]{:S(2)}) collective-permute-start(bf16[256,128]{1,0:T(8,128)(2,1)S(1)} %sides.1), channel_id=1, source_target_pairs={{128,0},{256,128},{384,256},{129,1},{257,129},{385,257},{130,2},{2... | collective-permute-start | bytes 196616 | tf_op jit(solution)/shard_map/ppermute | solution.py:199
  10.8 3.5 %collective-permute-start.4 = (bf16[256,128]{1,0:T(8,128)(2,1)S(1)}, bf16[256,128]{1,0:T(8,128)(2,1)S(1)}, u32[]{:S(2)}, u32[]{:S(2)}) collective-permute-start(bf16[256,128]{1,0:T(8,128)(2,1)S(1)} %sides.1), channel_id=1, source_target_pairs={{0,128},{128,256},{256,384},{1,129},{129,257},{257,385},{2,130},{1... | collective-permute-start | bytes 196616 | tf_op jit(solution)/shard_map/ppermute | solution.py:199
  14.3 1.9 %collective-permute-start.2 = (bf16[32,128]{1,0:T(8,128)(2,1)S(1)}, bf16[32,128]{1,0:T(8,128)(2,1)S(1)}, u32[]{:S(2)}, u32[]{:S(2)}) collective-permute-start(bf16[32,128]{1,0:T(8,128)(2,1)S(1)} %get-tuple-element.15), channel_id=1, source_target_pairs={{0,16},{16,32},{32,48},{48,64},{64,80},{80,96},{96,112},{1,17},{17... | collective-permute-start | bytes 24584 | tf_op jit(solution)/shard_map/ppermute | solution.py:199
  16.2 3.6 %collective-permute-start.3 = (bf16[32,128]{1,0:T(8,128)(2,1)S(1)}, bf16[32,128]{1,0:T(8,128)(2,1)S(1)}, u32[]{:S(2)}, u32[]{:S(2)}) collective-permute-start(bf16[32,128]{1,0:T(8,128)(2,1)S(1)} %get-tuple-element.16), channel_id=1, source_target_pairs={{16,0},{32,16},{48,32},{64,48},{80,64},{96,80},{112,96},{17,1},{33... | collective-permute-start | bytes 24584 | tf_op jit(solution)/shard_map/ppermute | solution.py:199
  19.9 0.1 copy.8.refs_0_
  20.0 0.0 copy-done.3
  20.0 2.8 %absorb.1 = (f32[32,256,128]{2,1,0:T(8,128)S(1)}, f32[256,128]{1,0:T(8,128)S(1)}) custom-call(f32[4,2]{1,0:T(4,128)S(1)} %copy.8.refs_0_, s32[32]{0:T(128)S(1)} %bitcast.5, bf16[32,256,128]{2,1,0:T(8,128)(2,1)S(1)} %copy-done.1, s32[256,128]{1,0:T(8,128)S(1)} %bitcast.3, s32[256,128]{1,0:T(8,128)S(1)} %bitcast.4), custom_call_target="tpu_custom_call" | custom-call | flops 12582912 | bytes 6291456 | tf_op jit(solution)/shard_map/absorb/pallas_call | solution.py:237
  22.9 0.0 collective-permute-done.2.refs_6_
  22.9 0.0 collective-permute-done.3.refs_7_
  22.9 0.0 collective-permute-done.1.refs_5_
  22.9 0.0 collective-permute-done.5.refs_9_
  22.9 0.0 collective-permute-done.4.refs_8_
  22.9 0.0 copy-start.2
  22.9 7.5 %shade.1 = s32[16,2,16,128]{3,2,1,0:T(8,128)S(1)} custom-call(f32[4,2]{1,0:T(4,128)S(1)} %copy.8.refs_0_, bf16[32,256,128]{2,1,0:T(8,128)(2,1)S(1)} %copy-done.1, f32[32,256,128]{2,1,0:T(8,128)S(1)} %get-tuple-element.11.refs_2_, f32[256,128]{1,0:T(8,128)S(1)} %get-tuple-element.12.refs_3_, bf16[256,128]{1,0:T(8,128)(2,1)S(1)} %collective-permute-done.arrived.refs_4_, ...), custom_call_target="tpu_custom_call" | custom-call | flops 41943040 | bytes 6291456 | tf_op jit(solution)/shard_map/shade/pallas_call | solution.py:249
  30.4 35.0 %all_to_all.10.parts = s32[16,2,16,128]{3,2,1,0:T(8,128)S(1)} all-to-all(s32[16,2,16,128]{3,2,1,0:T(8,128)S(1)} %shade.1), channel_id=1, replica_groups=mesh['tx'=4,'ty'=8,'depth'=16] {'depth'}, dimensions={0} | all-to-all | bytes 524288 | tf_op jit(solution)/shard_map/all_to_all | solution.py:262
  65.4 0.7 composite.1
  66.1 24.1 %all_to_all.11.words = s32[16,2,16,128]{3,2,1,0:T(8,128)S(1)} all-to-all(s32[16,2,16,128]{3,2,1,0:T(8,128)S(1)} %composite.1), channel_id=1, replica_groups=mesh['tx'=4,'ty'=8,'depth'=16] {'depth'}, dimensions={0} | all-to-all | bytes 524288 | tf_op jit(solution)/shard_map/all_to_all | solution.py:271
  90.2 0.9 frame.1
  (11 shorter events, 0.0 us)
Async XLA Ops:
  0.0 1.6 %copy-start = (bf16[32,256,128]{2,1,0:T(8,128)(2,1)S(1)}, bf16[32,256,128]{2,1,0:T(8,128)(2,1)}, u32[]{:S(2)}) copy-start(bf16[32,256,128]{2,1,0:T(8,128)(2,1)} %refs_1_.1) | copy-start | bytes 6291460
  1.6 18.3 %copy-start.6 = (f32[4,2]{0,1:T(2,128)S(1)}, f32[4,2]{0,1:T(2,128)}, u32[]{:S(2)}) copy-start(f32[4,2]{0,1:T(2,128)} %param.7) | copy-start | bytes 100
  1.6 18.4 %copy-start.1 = (bf16[32,256,128]{2,1,0:T(8,128)(2,1)S(1)}, bf16[32,256,128]{2,1,0:T(8,128)(2,1)}, u32[]{:S(2)}) copy-start(bf16[32,256,128]{2,1,0:T(8,128)(2,1)} %refs_1_.1) | copy-start | bytes 6291460
  1.6 18.4 %copy-start.3 = (s32[1,256,128]{2,1,0:T(8,128)S(1)}, s32[1,256,128]{2,1,0:T(8,128)}, u32[]{:S(2)}) copy-start(s32[1,256,128]{2,1,0:T(8,128)} %param.8) | copy-start | bytes 393220
  1.6 18.4 %copy-start.4 = (s32[1,256,128]{2,1,0:T(8,128)S(1)}, s32[1,256,128]{2,1,0:T(8,128)}, u32[]{:S(2)}) copy-start(s32[1,256,128]{2,1,0:T(8,128)} %param.9) | copy-start | bytes 393220
  1.6 18.4 %copy-start.5 = (s32[1,32,1]{1,2,0:T(1,128)S(1)}, s32[1,32,1]{1,2,0:T(1,128)}, u32[]{:S(2)}) copy-start(s32[1,32,1]{1,2,0:T(1,128)} %param.10) | copy-start | bytes 388
  1.9 5.8 %collective-permute-start = (bf16[256,128]{1,0:T(8,128)(2,1)S(1)}, bf16[256,128]{1,0:T(8,128)(2,1)S(1)}, u32[]{:S(2)}, u32[]{:S(2)}) collective-permute-start(bf16[256,128]{1,0:T(8,128)(2,1)S(1)} %get-tuple-element.13), channel_id=1, source_target_pairs={{0,1},{1,2},{2,3},{3,4},{4,5},{5,6},{6,7},{7,8},{8,9},{9,10},{10,1... | collective-permute-start | bytes 196616 | tf_op jit(solution)/shard_map/ppermute | solution.py:199
  5.9 17.0 %collective-permute-start.1 = (bf16[256,128]{1,0:T(8,128)(2,1)S(1)}, bf16[256,128]{1,0:T(8,128)(2,1)S(1)}, u32[]{:S(2)}, u32[]{:S(2)}) collective-permute-start(bf16[256,128]{1,0:T(8,128)(2,1)S(1)} %get-tuple-element.14), channel_id=1, source_target_pairs={{1,0},{2,1},{3,2},{4,3},{5,4},{6,5},{7,6},{8,7},{9,8},{10,9},{11,1... | collective-permute-start | bytes 196616 | tf_op jit(solution)/shard_map/ppermute | solution.py:199
  8.5 14.4 %collective-permute-start.5 = (bf16[256,128]{1,0:T(8,128)(2,1)S(1)}, bf16[256,128]{1,0:T(8,128)(2,1)S(1)}, u32[]{:S(2)}, u32[]{:S(2)}) collective-permute-start(bf16[256,128]{1,0:T(8,128)(2,1)S(1)} %sides.1), channel_id=1, source_target_pairs={{128,0},{256,128},{384,256},{129,1},{257,129},{385,257},{130,2},{2... | collective-permute-start | bytes 196616 | tf_op jit(solution)/shard_map/ppermute | solution.py:199
  10.8 12.1 %collective-permute-start.4 = (bf16[256,128]{1,0:T(8,128)(2,1)S(1)}, bf16[256,128]{1,0:T(8,128)(2,1)S(1)}, u32[]{:S(2)}, u32[]{:S(2)}) collective-permute-start(bf16[256,128]{1,0:T(8,128)(2,1)S(1)} %sides.1), channel_id=1, source_target_pairs={{0,128},{128,256},{256,384},{1,129},{129,257},{257,385},{2,130},{1... | collective-permute-start | bytes 196616 | tf_op jit(solution)/shard_map/ppermute | solution.py:199
  14.3 8.5 %collective-permute-start.2 = (bf16[32,128]{1,0:T(8,128)(2,1)S(1)}, bf16[32,128]{1,0:T(8,128)(2,1)S(1)}, u32[]{:S(2)}, u32[]{:S(2)}) collective-permute-start(bf16[32,128]{1,0:T(8,128)(2,1)S(1)} %get-tuple-element.15), channel_id=1, source_target_pairs={{0,16},{16,32},{32,48},{48,64},{64,80},{80,96},{96,112},{1,17},{17... | collective-permute-start | bytes 24584 | tf_op jit(solution)/shard_map/ppermute | solution.py:199
  16.2 6.6 %collective-permute-start.3 = (bf16[32,128]{1,0:T(8,128)(2,1)S(1)}, bf16[32,128]{1,0:T(8,128)(2,1)S(1)}, u32[]{:S(2)}, u32[]{:S(2)}) collective-permute-start(bf16[32,128]{1,0:T(8,128)(2,1)S(1)} %get-tuple-element.16), channel_id=1, source_target_pairs={{16,0},{32,16},{48,32},{64,48},{80,64},{96,80},{112,96},{17,1},{33... | collective-permute-start | bytes 24584 | tf_op jit(solution)/shard_map/ppermute | solution.py:199
  22.9 42.5 %copy-start.2 = (s32[16]{0:T(128)S(1)}, s32[16]{0:T(128)}, u32[]{:S(2)}) copy-start(s32[16]{0:T(128)} %order.1) | copy-start | bytes 196

commit v3 on v2

v3 whole, which is shorter than its diff:
```python
import jax
import jax.numpy as jnp
from jax import lax
from jax.experimental import pallas as pl
from jax.experimental.pallas import tpu as pltpu
from jax.sharding import PartitionSpec as P

LOG2E = 1.4426950408889634
CODE = 65535.0
PARTS = 2
VMEM = pltpu.VMEM
SMEM = pltpu.SMEM


def iota(shape, dim):
    return lax.broadcasted_iota(jnp.int32, shape, dim)


def encode(low, high):
    def code(x):
        root = jnp.sqrt(jnp.sqrt(jnp.maximum(x, 0.0)))
        return jnp.minimum(root * CODE + 0.5, CODE).astype(jnp.int32)

    return code(low) | (code(high) << 16)


def decode(word):
    def value(c):
        square = (c.astype(jnp.float32) * (1.0 / CODE)) ** 2
        return square * square

    return value(word & 0xFFFF), value(lax.shift_right_logical(word, 16))


def open_kernel(volume, start, stop, z0, z1, xt, field, begin, end, vol, sems):
    layers, rows, cols = vol.shape
    parts = sems.shape[0] - 2
    each = layers // parts
    copies = [
        pltpu.make_async_copy(
            volume.at[pl.ds(p * each, each)], vol.at[pl.ds(p * each, each)], sems.at[p]
        )
        for p in range(parts)
    ]
    copies.append(pltpu.make_async_copy(start, begin, sems.at[parts]))
    copies.append(pltpu.make_async_copy(stop, end, sems.at[parts + 1]))
    for copy in copies:
        copy.start()
    r, c = (iota((2 * cols, cols), 0), iota((2 * cols, cols), 1))
    column, second = (r % cols, r // cols)
    total = jnp.zeros((rows, cols), jnp.float32)
    for k in range(0, layers, 2):
        if k % each == 0:
            copies[k // each].wait()
        lane = 2 * (k + second)
        pick = ((column == 0) & (c == lane)) | ((column == cols - 1) & (c == (lane + cols - 1) % cols))
        one, two = (vol[k], vol[k + 1])
        field[k, 8 : rows + 8, :] = one.astype(jnp.float32)
        field[k + 1, 8 : rows + 8, :] = two.astype(jnp.float32)
        total = total + jnp.dot(
            jnp.concatenate([one, two], axis=1),
            pick.astype(jnp.float32).astype(jnp.bfloat16),
            preferred_element_type=jnp.float32,
        )
    z0[...] = vol[0]
    z1[...] = vol[layers - 1]
    xt[...] = total.astype(jnp.bfloat16)
    for copy in copies[parts:]:
        copy.wait()


def rows_kernel(field, arrived, y0, y1):
    rows = field.shape[1] - 16
    y0[...] = field[:, 8:16, :][:, 0, :].astype(jnp.bfloat16)
    y1[...] = field[:, rows : rows + 8, :][:, 7, :].astype(jnp.bfloat16)


def absorb_kernel(tf, pat, field, begin, end, weights, alpha, *, count, step_rows):
    layers, rows, cols = weights.shape
    f32 = jnp.float32
    slope, offset = (tf[0, 3] * LOG2E, tf[1, 3] * LOG2E)
    scale = -LOG2E * 2.0 / (layers * count)
    half = layers // 2

    def chunk(i, carry):
        base = pl.multiple_of(i * step_rows, step_rows)
        here = pl.ds(base, step_rows)
        middle = pl.ds(pl.multiple_of(base + 8, 8), step_rows)
        group = iota((step_rows, cols), 0) // 8
        on = jnp.zeros((step_rows, cols), jnp.int32)
        for g in range(step_rows // 8):
            on = jnp.where(group == g, pat[i * (step_rows // 8) + g], on)
        enter = jnp.where(on > 0, begin[here, :], layers)
        leave = jnp.where(on > 0, end[here, :], 0)
        depth = jnp.zeros((step_rows, cols), f32)
        before = depth + 1.0
        for k in range(layers):
            soft = jnp.log(1.0 + jnp.exp2(slope * field[k, middle, :] + offset))
            active = enter <= k if k < half else leave > k
            depth = depth + jnp.where(active, soft, 0.0)
            after = jnp.exp2(depth * scale)
            weights[k, here, :] = before - after
            before = after
        alpha[here, :] = 1.0 - before
        return carry

    lax.fori_loop(0, rows // step_rows, chunk, 0)


def shade_kernel(
    tf, middle_rows, weights, alpha, zlo, zhi, ylo, yhi, xlo, xhi, out, field, ends, *, count, step_rows
):
    del middle_rows
    layers, rows, cols = weights.shape
    f32 = jnp.float32
    sub = iota((layers, 8, cols), 1)
    field[:, 0:8, :] = jnp.where(sub == 7, ylo[...].astype(f32)[:, None, :], 0.0)
    field[:, rows + 8 : rows + 16, :] = jnp.where(sub == 0, yhi[...].astype(f32)[:, None, :], 0.0)

    slopes = [tf[0, j] * 0.5 for j in range(3)]
    offsets = [tf[1, j] * 0.5 for j in range(3)]
    strength = 0.64 * 0.7
    lane = iota((step_rows, cols), 1)
    first_lane, last_lane = (lane == 0, lane == cols - 1)

    def chunk(i, carry):
        base = pl.multiple_of(i * step_rows, step_rows)
        here = pl.ds(base, step_rows)
        middle = pl.ds(pl.multiple_of(base + 8, 8), step_rows)
        sides = jnp.where(lane % 2 == 0, xhi[here, :].astype(f32), xlo[here, :].astype(f32))
        for k in range(layers):
            ends[k] = sides if k == 0 else pltpu.roll(sides, cols - 2 * k, 1)
        zero = jnp.zeros((step_rows, cols), f32)
        shaded, tints = (zero, [zero, zero, zero])
        below, value = (zlo[here, :].astype(f32), field[0, middle, :])
        for k in range(layers):
            above = field[k + 1, middle, :] if k + 1 < layers else zhi[here, :].astype(f32)
            right = pltpu.roll(jnp.where(first_lane, ends[k], value), cols - 1, 1)
            left = pltpu.roll(jnp.where(last_lane, ends[k], value), 1, 1)
            sx, sz = (right - left, above - below)
            sy = field[k, pl.ds(base + 9, step_rows), :] - field[k, pl.ds(base + 7, step_rows), :]
            lit = jnp.abs((0.48 / 0.64) * sx + (0.6 / 0.64) * sy + sz)
            bright = lit * lax.rsqrt(sx * sx + sy * sy + sz * sz + 4.0) + 0.3 / strength
            weight = weights[k, here, :] * bright
            shaded = shaded + weight
            tints = [
                t + weight * jnp.tanh(s * value + o) for t, s, o in zip(tints, slopes, offsets)
            ]
            below, value = (value, above)
        red, green, blue = [(0.5 * strength) * (shaded + t) for t in tints]
        first, second = (encode(red, green), encode(blue, alpha[here, :]))
        share = rows // count
        for j in range(step_rows // share):
            out[i * (step_rows // share) + j, 0] = first[j * share : (j + 1) * share]
            out[i * (step_rows // share) + j, 1] = second[j * share : (j + 1) * share]
        return carry

    lax.fori_loop(0, rows // step_rows, chunk, 0)


def composite_kernel(order, parts, out):
    count, _, rows, cols = parts.shape

    def step(r, state):
        red, green, blue, left = state
        s = order[r]
        one, two = (decode(parts[s, 0]), decode(parts[s, 1]))
        return (red + left * one[0], green + left * one[1], blue + left * two[0], left * (1.0 - two[1]))

    zero = jnp.zeros((rows, cols), jnp.float32)
    state = (zero, zero, zero, zero + 1.0)
    for r in range(count):
        state = step(r, state)
    red, green, blue, left = state
    first, second = (encode(red, green), encode(blue, 1.0 - left))
    for s in range(count):
        out[s, 0] = first
        out[s, 1] = second


def frame_kernel(words, out):
    count, _, rows, cols = words.shape
    for s in range(count):
        here = slice(s * rows, (s + 1) * rows)
        for w in range(2):
            low, high = decode(words[s, w])
            out[2 * w, here, :] = low
            out[2 * w + 1, here, :] = high


def halo(array, axis, shift):
    count = lax.axis_size(axis)
    pairs = [(i, i + shift) for i in range(count) if 0 <= i + shift < count]
    return lax.ppermute(array, axis, pairs)


def shards(volume, transfer, ray_start, ray_stop, pattern, depth_order):
    layers, rows, cols = volume.shape
    count = lax.axis_size("depth")
    bf16, f32 = (jnp.bfloat16, jnp.float32)
    limit = pltpu.CompilerParams(vmem_limit_bytes=20 * 1024 * 1024)
    vmem = pl.BlockSpec(memory_space=VMEM)
    smem = pl.BlockSpec(memory_space=SMEM)
    shape = jax.ShapeDtypeStruct

    hbm = pl.BlockSpec(memory_space=pltpu.HBM)
    anywhere = pl.BlockSpec(memory_space=pl.ANY)

    whole = shape((rows, cols), bf16)
    bounds = shape((rows, cols), jnp.int32)
    z0, z1, xt, field, begin, end = pl.pallas_call(
        open_kernel,
        out_shape=[whole] * 3 + [shape((layers, rows + 16, cols), f32)] + [bounds] * 2,
        in_specs=[hbm] * 3,
        out_specs=[vmem] * 6,
        scratch_shapes=[VMEM(volume.shape, bf16), pltpu.SemaphoreType.DMA((PARTS + 2,))],
        compiler_params=limit,
        name="open",
    )(*[pltpu.with_memory_space_constraint(x, pltpu.HBM) for x in (volume, ray_start[0], ray_stop[0])])
    zlo, zhi = (halo(z1, "depth", 1), halo(z0, "depth", -1))
    xlo, xhi = (halo(xt, "tx", 1), halo(xt, "tx", -1))
    y0, y1 = pl.pallas_call(
        rows_kernel,
        out_shape=[shape((layers, cols), bf16)] * 2,
        in_specs=[vmem, anywhere],
        out_specs=[vmem] * 2,
        compiler_params=limit,
        name="rows",
    )(field, zlo)
    ylo, yhi = (halo(y1, "ty", 1), halo(y0, "ty", -1))

    step_rows = 32
    share = rows // count
    slopes = transfer.T
    weights, alpha = pl.pallas_call(
        lambda *refs: absorb_kernel(*refs, count=count, step_rows=step_rows),
        out_shape=[shape((layers, rows, cols), f32), shape((rows, cols), f32)],
        in_specs=[smem, smem] + [vmem] * 3,
        out_specs=[vmem] * 2,
        compiler_params=limit,
        cost_estimate=pl.CostEstimate(
            flops=12 * volume.size, bytes_accessed=8 * volume.size, transcendentals=3 * volume.size
        ),
        name="absorb",
    )(slopes, pattern.reshape(-1), field, begin, end)
    words, _ = pl.pallas_call(
        lambda *refs: shade_kernel(*refs, count=count, step_rows=step_rows),
        out_shape=[shape((count, 2, share, cols), jnp.int32), shape(field.shape, f32)],
        in_specs=[smem] + [vmem] * 9,
        out_specs=[vmem] * 2,
        scratch_shapes=[VMEM((layers, step_rows, cols), f32)],
        input_output_aliases={1: 1},
        compiler_params=limit,
        cost_estimate=pl.CostEstimate(
            flops=40 * volume.size, bytes_accessed=8 * volume.size, transcendentals=4 * volume.size
        ),
        name="shade",
    )(slopes, field, weights, alpha, zlo, zhi, ylo, yhi, xlo, xhi)

    words = lax.all_to_all(words, "depth", split_axis=0, concat_axis=0, tiled=True)
    words = pl.pallas_call(
        composite_kernel,
        out_shape=shape(words.shape, jnp.int32),
        in_specs=[smem, vmem],
        out_specs=vmem,
        compiler_params=limit,
        name="composite",
    )(depth_order, words)
    words = lax.all_to_all(words, "depth", split_axis=0, concat_axis=0, tiled=True)
    return pl.pallas_call(
        frame_kernel,
        out_shape=shape((4, rows, cols), f32),
        in_specs=[vmem],
        out_specs=vmem,
        compiler_params=limit,
        name="frame",
    )(words)


def solution(mesh):
    in_specs = (
        P("depth", "ty", "tx"),
        P(),
        P("depth", "ty", "tx"),
        P("depth", "ty", "tx"),
        P("depth", "ty", "tx"),
        P(),
    )
    out_specs = P(None, "ty", "tx")
    return jax.shard_map(shards, mesh=mesh, in_specs=in_specs, out_specs=out_specs, check_vma=False)
```

time: 91.4 us -> 90.1 us (0.986)
  the two profiles are of different devices: /device:TPU:18 before, /device:TPU:10 now
where the time goes in v3:
time: 90.1 us; the launch traced here: 89.7 us
  blocking collectives  59.9 us (66%)
  starting transfers between devices  16.5 us (18%)
  Pallas kernels  13.1 us (15%)
    all_to_all x2, blocking collectives, shards(): lax.all_to_all(words, 'depth', split_axis=0, concat_axis=0, tiled=True)  59.9 us
    ppermute x6, starting transfers between devices, halo(): return lax.ppermute(array, axis, pairs)  16.5 us
    pallas_call x1, Pallas kernels, shards(): pl.pallas_call(lambda *refs: shade_kernel(*refs, count=count, step_rows=s...  6.95 us
    pallas_call x1, Pallas kernels, shards(): pl.pallas_call(lambda *refs: absorb_kernel(*refs, count=count, step_rows=...  2.4 us
    pallas_call x1, Pallas kernels, shards(): pl.pallas_call(open_kernel, out_shape=[whole] * 3 + [shape((layers, rows...  2.17 us
  transfers between devices with their start and end apart: 6, of which 0 were waited for; matrix products, arithmetic and copies ran while one was open for 0% of the time, Pallas kernels for 3%

profile of v3, /device:TPU:10, one launch (start us, length us, event | category | flops | bytes accessed | tf_op | source)
XLA Modules:
  0.0 89.7 jit_solution(5111193292982716528)
XLA Ops:
  0.0 0.0 copy-start.2
  0.0 2.2 %open.1 = (bf16[256,128]{1,0:T(8,128)(2,1)S(1)}, bf16[256,128]{1,0:T(8,128)(2,1)S(1)}, bf16[256,128]{1,0:T(8,128)(2,1)S(1)}, f32[32,272,128]{2,1,0:T(8,128)S(1)}...) custom-call(bf16[32,256,128]{2,1,0:T(8,128)(2,1)} %volume.1, s32[256,128]{1,0:T(8,128)} %bitcast.7, s32[256,128]{1,0:T(8,128)} %bitcast.8), custom_call_target="tpu_custom_call" | custom-call | tf_op jit(solution)/shard_map/open/pallas_call | solution.py:211
  2.2 3.8 %collective-permute-start = (bf16[256,128]{1,0:T(8,128)(2,1)S(1)}, bf16[256,128]{1,0:T(8,128)(2,1)S(1)}, u32[]{:S(2)}, u32[]{:S(2)}) collective-permute-start(bf16[256,128]{1,0:T(8,128)(2,1)S(1)} %get-tuple-element.21), channel_id=1, source_target_pairs={{0,1},{1,2},{2,3},{3,4},{4,5},{5,6},{6,7},{7,8},{8,9},{9,10},{10,1... | collective-permute-start | bytes 196616 | tf_op jit(solution)/shard_map/ppermute | solution.py:194
  6.0 1.3 %collective-permute-start.1 = (bf16[256,128]{1,0:T(8,128)(2,1)S(1)}, bf16[256,128]{1,0:T(8,128)(2,1)S(1)}, u32[]{:S(2)}, u32[]{:S(2)}) collective-permute-start(bf16[256,128]{1,0:T(8,128)(2,1)S(1)} %get-tuple-element.22), channel_id=1, source_target_pairs={{1,0},{2,1},{3,2},{4,3},{5,4},{6,5},{7,6},{8,7},{9,8},{10,9},{11,1... | collective-permute-start | bytes 196616 | tf_op jit(solution)/shard_map/ppermute | solution.py:194
  7.3 2.4 %collective-permute-start.5 = (bf16[256,128]{1,0:T(8,128)(2,1)S(1)}, bf16[256,128]{1,0:T(8,128)(2,1)S(1)}, u32[]{:S(2)}, u32[]{:S(2)}) collective-permute-start(bf16[256,128]{1,0:T(8,128)(2,1)S(1)} %get-tuple-element.25), channel_id=1, source_target_pairs={{128,0},{256,128},{384,256},{129,1},{257,129},{385,257},{130,2},{2... | collective-permute-start | bytes 196616 | tf_op jit(solution)/shard_map/ppermute | solution.py:194
  9.7 3.5 %collective-permute-start.4 = (bf16[256,128]{1,0:T(8,128)(2,1)S(1)}, bf16[256,128]{1,0:T(8,128)(2,1)S(1)}, u32[]{:S(2)}, u32[]{:S(2)}) collective-permute-start(bf16[256,128]{1,0:T(8,128)(2,1)S(1)} %get-tuple-element.25), channel_id=1, source_target_pairs={{0,128},{128,256},{256,384},{1,129},{129,257},{257,385},{2,130},{1... | collective-permute-start | bytes 196616 | tf_op jit(solution)/shard_map/ppermute | solution.py:194
  13.2 0.0 collective-permute-done.arrived.refs_4_
  13.2 1.9 %collective-permute-start.2 = (bf16[32,128]{1,0:T(8,128)(2,1)S(1)}, bf16[32,128]{1,0:T(8,128)(2,1)S(1)}, u32[]{:S(2)}, u32[]{:S(2)}) collective-permute-start(bf16[32,128]{1,0:T(8,128)(2,1)S(1)} %get-tuple-element.23), channel_id=1, source_target_pairs={{0,16},{16,32},{32,48},{48,64},{64,80},{80,96},{96,112},{1,17},{17... | collective-permute-start | bytes 24584 | tf_op jit(solution)/shard_map/ppermute | solution.py:194
  15.2 3.6 %collective-permute-start.3 = (bf16[32,128]{1,0:T(8,128)(2,1)S(1)}, bf16[32,128]{1,0:T(8,128)(2,1)S(1)}, u32[]{:S(2)}, u32[]{:S(2)}) collective-permute-start(bf16[32,128]{1,0:T(8,128)(2,1)S(1)} %get-tuple-element.24), channel_id=1, source_target_pairs={{16,0},{32,16},{48,32},{64,48},{80,64},{96,80},{112,96},{17,1},{33... | collective-permute-start | bytes 24584 | tf_op jit(solution)/shard_map/ppermute | solution.py:194
  18.8 0.0 copy-done.2
  18.8 0.0 copy-done
  18.8 2.4 %absorb.1 = (f32[32,256,128]{2,1,0:T(8,128)S(1)}, f32[256,128]{1,0:T(8,128)S(1)}) custom-call(f32[2,4]{1,0:T(2,128)S(1)} %bitcast.4, s32[32]{0:T(128)S(1)} %bitcast.6, f32[32,272,128]{2,1,0:T(8,128)S(1)} %get-tuple-element.16.refs_2_.field.refs_1_, s32[256,128]{1,0:T(8,128)S(1)} %get-tuple-element.17.refs_3_, s32[256,128]{1,0:T(8,128)S(1)} %get-tuple-element.18.refs_4_), custom_call_target="tpu_custom_call" | custom-call | flops 12582912 | bytes 8388608 | tf_op jit(solution)/shard_map/absorb/pallas_call | solution.py:235
  21.2 0.0 collective-permute-done.1.refs_5_
  21.2 0.0 collective-permute-done.5.refs_9_
  21.2 0.0 collective-permute-done.4.refs_8_
  21.3 0.0 collective-permute-done.2.refs_6_
  21.3 0.0 collective-permute-done.3.refs_7_
  21.3 0.0 copy-start.1
  21.3 6.9 %shade.1 = (s32[16,2,16,128]{3,2,1,0:T(8,128)S(1)}, f32[32,272,128]{2,1,0:T(8,128)S(1)}) custom-call(f32[2,4]{1,0:T(2,128)S(1)} %bitcast.5, f32[32,272,128]{2,1,0:T(8,128)S(1)} %get-tuple-element.16.refs_2_.field.refs_1_, f32[32,256,128]{2,1,0:T(8,128)S(1)} %get-tuple-element.19.refs_2_, ...), custom_call_target="tpu_custom_call", output_to_operand_aliasing={{1}: (1, {})} | custom-call | flops 41943040 | bytes 8388608 | tf_op jit(solution)/shard_map/shade/pallas_call | solution.py:246
  28.3 35.7 %all_to_all.10.parts = s32[16,2,16,128]{3,2,1,0:T(8,128)S(1)} all-to-all(s32[16,2,16,128]{3,2,1,0:T(8,128)S(1)} %get-tuple-element.26), channel_id=1, replica_groups=mesh['tx'=4,'ty'=8,'depth'=16] {'depth'}, dimensions={0} | all-to-all | bytes 524288 | tf_op jit(solution)/shard_map/all_to_all | solution.py:260
  64.0 0.0 copy-done.1
  64.0 0.7 composite.1
  64.7 24.1 %all_to_all.11.words = s32[16,2,16,128]{3,2,1,0:T(8,128)S(1)} all-to-all(s32[16,2,16,128]{3,2,1,0:T(8,128)S(1)} %composite.1), channel_id=1, replica_groups=mesh['tx'=4,'ty'=8,'depth'=16] {'depth'}, dimensions={0} | all-to-all | bytes 524288 | tf_op jit(solution)/shard_map/all_to_all | solution.py:269
  88.8 0.9 frame.1
  (2 shorter events, 0.0 us)
Async XLA Ops:
  0.0 18.8 %copy-start.2 = (s32[1,32,1]{1,2,0:T(1,128)S(1)}, s32[1,32,1]{1,2,0:T(1,128)}, u32[]{:S(2)}) copy-start(s32[1,32,1]{1,2,0:T(1,128)} %param.10) | copy-start | bytes 388
  0.0 18.8 %copy-start = (f32[4,2]{0,1:T(2,128)S(1)}, f32[4,2]{0,1:T(2,128)}, u32[]{:S(2)}) copy-start(f32[4,2]{0,1:T(2,128)} %param.7) | copy-start | bytes 100
  2.2 11.0 %collective-permute-start = (bf16[256,128]{1,0:T(8,128)(2,1)S(1)}, bf16[256,128]{1,0:T(8,128)(2,1)S(1)}, u32[]{:S(2)}, u32[]{:S(2)}) collective-permute-start(bf16[256,128]{1,0:T(8,128)(2,1)S(1)} %get-tuple-element.21), channel_id=1, source_target_pairs={{0,1},{1,2},{2,3},{3,4},{4,5},{5,6},{6,7},{7,8},{8,9},{9,10},{10,1... | collective-permute-start | bytes 196616 | tf_op jit(solution)/shard_map/ppermute | solution.py:194
  6.0 15.2 %collective-permute-start.1 = (bf16[256,128]{1,0:T(8,128)(2,1)S(1)}, bf16[256,128]{1,0:T(8,128)(2,1)S(1)}, u32[]{:S(2)}, u32[]{:S(2)}) collective-permute-start(bf16[256,128]{1,0:T(8,128)(2,1)S(1)} %get-tuple-element.22), channel_id=1, source_target_pairs={{1,0},{2,1},{3,2},{4,3},{5,4},{6,5},{7,6},{8,7},{9,8},{10,9},{11,1... | collective-permute-start | bytes 196616 | tf_op jit(solution)/shard_map/ppermute | solution.py:194
  7.3 13.9 %collective-permute-start.5 = (bf16[256,128]{1,0:T(8,128)(2,1)S(1)}, bf16[256,128]{1,0:T(8,128)(2,1)S(1)}, u32[]{:S(2)}, u32[]{:S(2)}) collective-permute-start(bf16[256,128]{1,0:T(8,128)(2,1)S(1)} %get-tuple-element.25), channel_id=1, source_target_pairs={{128,0},{256,128},{384,256},{129,1},{257,129},{385,257},{130,2},{2... | collective-permute-start | bytes 196616 | tf_op jit(solution)/shard_map/ppermute | solution.py:194
  9.7 11.6 %collective-permute-start.4 = (bf16[256,128]{1,0:T(8,128)(2,1)S(1)}, bf16[256,128]{1,0:T(8,128)(2,1)S(1)}, u32[]{:S(2)}, u32[]{:S(2)}) collective-permute-start(bf16[256,128]{1,0:T(8,128)(2,1)S(1)} %get-tuple-element.25), channel_id=1, source_target_pairs={{0,128},{128,256},{256,384},{1,129},{129,257},{257,385},{2,130},{1... | collective-permute-start | bytes 196616 | tf_op jit(solution)/shard_map/ppermute | solution.py:194
  13.2 8.0 %collective-permute-start.2 = (bf16[32,128]{1,0:T(8,128)(2,1)S(1)}, bf16[32,128]{1,0:T(8,128)(2,1)S(1)}, u32[]{:S(2)}, u32[]{:S(2)}) collective-permute-start(bf16[32,128]{1,0:T(8,128)(2,1)S(1)} %get-tuple-element.23), channel_id=1, source_target_pairs={{0,16},{16,32},{32,48},{48,64},{64,80},{80,96},{96,112},{1,17},{17... | collective-permute-start | bytes 24584 | tf_op jit(solution)/shard_map/ppermute | solution.py:194
  15.2 6.1 %collective-permute-start.3 = (bf16[32,128]{1,0:T(8,128)(2,1)S(1)}, bf16[32,128]{1,0:T(8,128)(2,1)S(1)}, u32[]{:S(2)}, u32[]{:S(2)}) collective-permute-start(bf16[32,128]{1,0:T(8,128)(2,1)S(1)} %get-tuple-element.24), channel_id=1, source_target_pairs={{16,0},{32,16},{48,32},{64,48},{80,64},{96,80},{112,96},{17,1},{33... | collective-permute-start | bytes 24584 | tf_op jit(solution)/shard_map/ppermute | solution.py:194
  21.3 42.7 %copy-start.1 = (s32[16]{0:T(128)S(1)}, s32[16]{0:T(128)}, u32[]{:S(2)}) copy-start(s32[16]{0:T(128)} %order.1) | copy-start | bytes 196

commit v4 on v3

--- a/solution.py
+++ b/solution.py
@@ -32,7 +32,7 @@
     return value(word & 0xFFFF), value(lax.shift_right_logical(word, 16))
 
 
-def open_kernel(volume, start, stop, z0, z1, xt, field, begin, end, vol, sems):
+def open_kernel(volume, start, stop, z0, z1, xt, field, begin, end, near, vol, sems):
     layers, rows, cols = vol.shape
     parts = sems.shape[0] - 2
     each = layers // parts
@@ -46,6 +46,7 @@
     copies.append(pltpu.make_async_copy(stop, end, sems.at[parts + 1]))
     for copy in copies:
         copy.start()
+    near[...] = neighbours()
     r, c = (iota((2 * cols, cols), 0), iota((2 * cols, cols), 1))
     column, second = (r % cols, r // cols)
     total = jnp.zeros((rows, cols), jnp.float32)
@@ -108,14 +109,19 @@
 
 
 def shade_kernel(
-    tf, middle_rows, weights, alpha, zlo, zhi, ylo, yhi, xlo, xhi, out, field, ends, *, count, step_rows
+    tf, middle_rows, weights, alpha, near, zlo, zhi, ylo, yhi, xlo, xhi, out, field, ends,
+    *, count, step_rows
 ):
     del middle_rows
     layers, rows, cols = weights.shape
     f32 = jnp.float32
     sub = iota((layers, 8, cols), 1)
-    field[:, 0:8, :] = jnp.where(sub == 7, ylo[...].astype(f32)[:, None, :], 0.0)
-    field[:, rows + 8 : rows + 16, :] = jnp.where(sub == 0, yhi[...].astype(f32)[:, None, :], 0.0)
+    kept = {axis: (near[2 * i : 2 * i + 1, :], near[2 * i + 1 : 2 * i + 2, :]) for i, axis in enumerate(AXES)}
+    low, high = kept["ty"]
+    field[:, 0:8, :] = jnp.where(sub == 7, (ylo[...].astype(f32) * low)[:, None, :], 0.0)
+    field[:, rows + 8 : rows + 16, :] = jnp.where(
+        sub == 0, (yhi[...].astype(f32) * high)[:, None, :], 0.0
+    )
 
     slopes = [tf[0, j] * 0.5 for j in range(3)]
     offsets = [tf[1, j] * 0.5 for j in range(3)]
@@ -127,14 +133,18 @@
         base = pl.multiple_of(i * step_rows, step_rows)
         here = pl.ds(base, step_rows)
         middle = pl.ds(pl.multiple_of(base + 8, 8), step_rows)
-        sides = jnp.where(lane % 2 == 0, xhi[here, :].astype(f32), xlo[here, :].astype(f32))
+        low, high = kept["tx"]
+        sides = jnp.where(
+            lane % 2 == 0, xhi[here, :].astype(f32) * high, xlo[here, :].astype(f32) * low
+        )
         for k in range(layers):
             ends[k] = sides if k == 0 else pltpu.roll(sides, cols - 2 * k, 1)
         zero = jnp.zeros((step_rows, cols), f32)
         shaded, tints = (zero, [zero, zero, zero])
-        below, value = (zlo[here, :].astype(f32), field[0, middle, :])
+        low, high = kept["depth"]
+        below, value = (zlo[here, :].astype(f32) * low, field[0, middle, :])
         for k in range(layers):
-            above = field[k + 1, middle, :] if k + 1 < layers else zhi[here, :].astype(f32)
+            above = field[k + 1, middle, :] if k + 1 < layers else zhi[here, :].astype(f32) * high
             right = pltpu.roll(jnp.where(first_lane, ends[k], value), cols - 1, 1)
             left = pltpu.roll(jnp.where(last_lane, ends[k], value), 1, 1)
             sx, sz = (right - left, above - below)
@@ -190,8 +200,20 @@
 
 def halo(array, axis, shift):
     count = lax.axis_size(axis)
-    pairs = [(i, i + shift) for i in range(count) if 0 <= i + shift < count]
-    return lax.ppermute(array, axis, pairs)
+    return lax.ppermute(array, axis, [(i, (i + shift) % count) for i in range(count)])
+
+
+AXES = ("tx", "ty", "depth")
+
+
+def neighbours():
+    row = iota((8, 128), 0)
+    flags = jnp.zeros((8, 128), jnp.float32)
+    for i, axis in enumerate(AXES):
+        place, count = (lax.axis_index(axis), lax.axis_size(axis))
+        flags = jnp.where(row == 2 * i, (place > 0).astype(jnp.float32), flags)
+        flags = jnp.where(row == 2 * i + 1, (place < count - 1).astype(jnp.float32), flags)
+    return flags
 
 
 def shards(volume, transfer, ray_start, ray_stop, pattern, depth_order):
@@ -208,11 +230,11 @@
 
     whole = shape((rows, cols), bf16)
     bounds = shape((rows, cols), jnp.int32)
-    z0, z1, xt, field, begin, end = pl.pallas_call(
+    z0, z1, xt, field, begin, end, near = pl.pallas_call(
         open_kernel,
-        out_shape=[whole] * 3 + [shape((layers, rows + 16, cols), f32)] + [bounds] * 2,
+        out_shape=[whole] * 3 + [shape((layers, rows + 16, cols), f32)] + [bounds] * 2 + [shape((8, 128), f32)],
         in_specs=[hbm] * 3,
-        out_specs=[vmem] * 6,
+        out_specs=[vmem] * 7,
         scratch_shapes=[VMEM(volume.shape, bf16), pltpu.SemaphoreType.DMA((PARTS + 2,))],
         compiler_params=limit,
         name="open",
@@ -246,7 +268,7 @@
     words, _ = pl.pallas_call(
         lambda *refs: shade_kernel(*refs, count=count, step_rows=step_rows),
         out_shape=[shape((count, 2, share, cols), jnp.int32), shape(field.shape, f32)],
-        in_specs=[smem] + [vmem] * 9,
+        in_specs=[smem] + [vmem] * 10,
         out_specs=[vmem] * 2,
         scratch_shapes=[VMEM((layers, step_rows, cols), f32)],
         input_output_aliases={1: 1},
@@ -255,7 +277,7 @@
             flops=40 * volume.size, bytes_accessed=8 * volume.size, transcendentals=4 * volume.size
         ),
         name="shade",
-    )(slopes, field, weights, alpha, zlo, zhi, ylo, yhi, xlo, xhi)
+    )(slopes, field, weights, alpha, near, zlo, zhi, ylo, yhi, xlo, xhi)
 
     words = lax.all_to_all(words, "depth", split_axis=0, concat_axis=0, tiled=True)
     words = pl.pallas_call(

time: 90.1 us -> 88.4 us (0.981)
  the two profiles are of different devices: /device:TPU:10 before, /device:TPU:6 now
where the time goes in v4:
time: 88.4 us; the launch traced here: 88.1 us
  blocking collectives  51 us (58%)
  starting transfers between devices  21.9 us (25%)
  Pallas kernels  13.8 us (16%)
  waiting for transfers between devices  1.21 us (1%)
    all_to_all x2, blocking collectives, shards(): lax.all_to_all(words, 'depth', split_axis=0, concat_axis=0, tiled=True)  51 us
    ppermute x6, starting transfers between devices, halo(): lax.ppermute(array, axis, [(i, (i + shift) % count) for i in range(count)])  21.9 us
    pallas_call x1, Pallas kernels, shards(): pl.pallas_call(lambda *refs: shade_kernel(*refs, count=count, step_rows=s...  7.61 us
    pallas_call x1, Pallas kernels, shards(): pl.pallas_call(lambda *refs: absorb_kernel(*refs, count=count, step_rows=...  2.39 us
    pallas_call x1, Pallas kernels, shards(): pl.pallas_call(open_kernel, out_shape=[whole] * 3 + [shape((layers, rows...  2.17 us
  transfers between devices with their start and end apart: 6, of which 1 were waited for; matrix products, arithmetic and copies ran while one was open for 0% of the time, Pallas kernels for 3%

profile of v4, /device:TPU:6, one launch (start us, length us, event | category | flops | bytes accessed | tf_op | source)
XLA Modules:
  0.0 88.1 jit_solution(13381167130374201450)
XLA Ops:
  0.0 0.0 copy-start.2
  0.0 0.0 copy-start
  0.0 2.2 %open.1 = (bf16[256,128]{1,0:T(8,128)(2,1)S(1)}, bf16[256,128]{1,0:T(8,128)(2,1)S(1)}, bf16[256,128]{1,0:T(8,128)(2,1)S(1)}, f32[32,272,128]{2,1,0:T(8,128)S(1)}...) custom-call(bf16[32,256,128]{2,1,0:T(8,128)(2,1)} %volume.1, s32[256,128]{1,0:T(8,128)} %bitcast.7, ...), custom_call_target="tpu_custom_call" | custom-call | tf_op jit(solution)/shard_map/open/pallas_call | solution.py:233
  2.2 3.8 %collective-permute-start = (bf16[256,128]{1,0:T(8,128)(2,1)S(1)}, bf16[256,128]{1,0:T(8,128)(2,1)S(1)}, u32[]{:S(2)}, u32[]{:S(2)}) collective-permute-start(bf16[256,128]{1,0:T(8,128)(2,1)S(1)} %get-tuple-element.23), channel_id=1, source_target_pairs={{0,1},{1,2},{2,3},{3,4},{4,5},{5,6},{6,7},{7,8},{8,9},{9,10},{10,1... | collective-permute-start | bytes 196616 | tf_op jit(solution)/shard_map/ppermute | solution.py:203
  6.0 9.5 %collective-permute-start.1 = (bf16[256,128]{1,0:T(8,128)(2,1)S(1)}, bf16[256,128]{1,0:T(8,128)(2,1)S(1)}, u32[]{:S(2)}, u32[]{:S(2)}) collective-permute-start(bf16[256,128]{1,0:T(8,128)(2,1)S(1)} %get-tuple-element.24), channel_id=1, source_target_pairs={{0,15},{1,0},{2,1},{3,2},{4,3},{5,4},{6,5},{7,6},{8,7},{9,8},{10,9... | collective-permute-start | bytes 196616 | tf_op jit(solution)/shard_map/ppermute | solution.py:203
  15.5 4.9 %collective-permute-start.5 = (bf16[256,128]{1,0:T(8,128)(2,1)S(1)}, bf16[256,128]{1,0:T(8,128)(2,1)S(1)}, u32[]{:S(2)}, u32[]{:S(2)}) collective-permute-start(bf16[256,128]{1,0:T(8,128)(2,1)S(1)} %get-tuple-element.27), channel_id=1, source_target_pairs={{0,384},{128,0},{256,128},{384,256},{1,385},{129,1},{257,129},{385... | collective-permute-start | bytes 196616 | tf_op jit(solution)/shard_map/ppermute | solution.py:203
  20.5 1.9 %collective-permute-start.4 = (bf16[256,128]{1,0:T(8,128)(2,1)S(1)}, bf16[256,128]{1,0:T(8,128)(2,1)S(1)}, u32[]{:S(2)}, u32[]{:S(2)}) collective-permute-start(bf16[256,128]{1,0:T(8,128)(2,1)S(1)} %get-tuple-element.27), channel_id=1, source_target_pairs={{0,128},{128,256},{256,384},{384,0},{1,129},{129,257},{257,385},{3... | collective-permute-start | bytes 196616 | tf_op jit(solution)/shard_map/ppermute | solution.py:203
  22.4 0.0 collective-permute-done.arrived.refs_5_
  22.4 0.0 collective-permute-start.2
  22.5 1.7 %collective-permute-start.3 = (bf16[32,128]{1,0:T(8,128)(2,1)S(1)}, bf16[32,128]{1,0:T(8,128)(2,1)S(1)}, u32[]{:S(2)}, u32[]{:S(2)}) collective-permute-start(bf16[32,128]{1,0:T(8,128)(2,1)S(1)} %get-tuple-element.26), channel_id=1, source_target_pairs={{0,112},{16,0},{32,16},{48,32},{64,48},{80,64},{96,80},{112,96},{1... | collective-permute-start | bytes 24584 | tf_op jit(solution)/shard_map/ppermute | solution.py:203
  24.2 0.0 copy-done.2
  24.2 0.0 copy-done
  24.2 2.4 %absorb.1 = (f32[32,256,128]{2,1,0:T(8,128)S(1)}, f32[256,128]{1,0:T(8,128)S(1)}) custom-call(f32[2,4]{1,0:T(2,128)S(1)} %bitcast.4, s32[32]{0:T(128)S(1)} %bitcast.6, f32[32,272,128]{2,1,0:T(8,128)S(1)} %get-tuple-element.17.refs_2_.field.refs_1_, s32[256,128]{1,0:T(8,128)S(1)} %get-tuple-element.18.refs_3_, s32[256,128]{1,0:T(8,128)S(1)} %get-tuple-element.19.refs_4_), custom_call_target="tpu_custom_call" | custom-call | flops 12582912 | bytes 8388608 | tf_op jit(solution)/shard_map/absorb/pallas_call | solution.py:257
  26.6 0.0 collective-permute-done.1.refs_6_
  26.6 0.0 collective-permute-done.5.refs_10_
  26.6 1.2 %collective-permute-done.4.refs_9_ = bf16[256,128]{1,0:T(8,128)(2,1)S(1)} collective-permute-done((bf16[256,128]{1,0:T(8,128)(2,1)S(1)}, bf16[256,128]{1,0:T(8,128)(2,1)S(1)}, u32[]{:S(2)}, u32[]{:S(2)}) %collective-permute-start.4) | collective-permute-done | bytes 65568 | tf_op jit(solution)/shard_map/ppermute | solution.py:203
  27.8 0.0 collective-permute-done.2.refs_7_
  27.8 0.0 collective-permute-done.3.refs_8_
  27.8 7.6 %shade.1 = (s32[16,2,16,128]{3,2,1,0:T(8,128)S(1)}, f32[32,272,128]{2,1,0:T(8,128)S(1)}) custom-call(f32[2,4]{1,0:T(2,128)S(1)} %bitcast.5, f32[32,272,128]{2,1,0:T(8,128)S(1)} %get-tuple-element.17.refs_2_.field.refs_1_, f32[32,256,128]{2,1,0:T(8,128)S(1)} %get-tuple-element.20.refs_2_, ...), custom_call_target="tpu_custom_call", output_to_operand_aliasing={{1}: (1, {})} | custom-call | flops 41943040 | bytes 8388608 | tf_op jit(solution)/shard_map/shade/pallas_call | solution.py:268
  35.4 27.1 %all_to_all.10.parts = s32[16,2,16,128]{3,2,1,0:T(8,128)S(1)} all-to-all(s32[16,2,16,128]{3,2,1,0:T(8,128)S(1)} %get-tuple-element.28), channel_id=1, replica_groups=mesh['tx'=4,'ty'=8,'depth'=16] {'depth'}, dimensions={0} | all-to-all | bytes 524288 | tf_op jit(solution)/shard_map/all_to_all | solution.py:282
  62.6 0.0 copy-done.1
  62.6 0.7 composite.1
  63.3 23.9 %all_to_all.11.words = s32[16,2,16,128]{3,2,1,0:T(8,128)S(1)} all-to-all(s32[16,2,16,128]{3,2,1,0:T(8,128)S(1)} %composite.1), channel_id=1, replica_groups=mesh['tx'=4,'ty'=8,'depth'=16] {'depth'}, dimensions={0} | all-to-all | bytes 524288 | tf_op jit(solution)/shard_map/all_to_all | solution.py:291
  87.2 0.9 frame.1
  (2 shorter events, 0.0 us)
Async XLA Ops:
  0.0 24.2 %copy-start.2 = (s32[1,32,1]{1,2,0:T(1,128)S(1)}, s32[1,32,1]{1,2,0:T(1,128)}, u32[]{:S(2)}) copy-start(s32[1,32,1]{1,2,0:T(1,128)} %param.10) | copy-start | bytes 388
  0.0 24.2 %copy-start = (f32[4,2]{0,1:T(2,128)S(1)}, f32[4,2]{0,1:T(2,128)}, u32[]{:S(2)}) copy-start(f32[4,2]{0,1:T(2,128)} %param.7) | copy-start | bytes 100
  2.2 20.2 %collective-permute-start = (bf16[256,128]{1,0:T(8,128)(2,1)S(1)}, bf16[256,128]{1,0:T(8,128)(2,1)S(1)}, u32[]{:S(2)}, u32[]{:S(2)}) collective-permute-start(bf16[256,128]{1,0:T(8,128)(2,1)S(1)} %get-tuple-element.23), channel_id=1, source_target_pairs={{0,1},{1,2},{2,3},{3,4},{4,5},{5,6},{6,7},{7,8},{8,9},{9,10},{10,1... | collective-permute-start | bytes 196616 | tf_op jit(solution)/shard_map/ppermute | solution.py:203
  6.0 20.6 %collective-permute-start.1 = (bf16[256,128]{1,0:T(8,128)(2,1)S(1)}, bf16[256,128]{1,0:T(8,128)(2,1)S(1)}, u32[]{:S(2)}, u32[]{:S(2)}) collective-permute-start(bf16[256,128]{1,0:T(8,128)(2,1)S(1)} %get-tuple-element.24), channel_id=1, source_target_pairs={{0,15},{1,0},{2,1},{3,2},{4,3},{5,4},{6,5},{7,6},{8,7},{9,8},{10,9... | collective-permute-start | bytes 196616 | tf_op jit(solution)/shard_map/ppermute | solution.py:203
  15.5 11.1 %collective-permute-start.5 = (bf16[256,128]{1,0:T(8,128)(2,1)S(1)}, bf16[256,128]{1,0:T(8,128)(2,1)S(1)}, u32[]{:S(2)}, u32[]{:S(2)}) collective-permute-start(bf16[256,128]{1,0:T(8,128)(2,1)S(1)} %get-tuple-element.27), channel_id=1, source_target_pairs={{0,384},{128,0},{256,128},{384,256},{1,385},{129,1},{257,129},{385... | collective-permute-start | bytes 196616 | tf_op jit(solution)/shard_map/ppermute | solution.py:203
  20.5 7.4 %collective-permute-start.4 = (bf16[256,128]{1,0:T(8,128)(2,1)S(1)}, bf16[256,128]{1,0:T(8,128)(2,1)S(1)}, u32[]{:S(2)}, u32[]{:S(2)}) collective-permute-start(bf16[256,128]{1,0:T(8,128)(2,1)S(1)} %get-tuple-element.27), channel_id=1, source_target_pairs={{0,128},{128,256},{256,384},{384,0},{1,129},{129,257},{257,385},{3... | collective-permute-start | bytes 196616 | tf_op jit(solution)/shard_map/ppermute | solution.py:203
  22.4 5.4 %collective-permute-start.2 = (bf16[32,128]{1,0:T(8,128)(2,1)S(1)}, bf16[32,128]{1,0:T(8,128)(2,1)S(1)}, u32[]{:S(2)}, u32[]{:S(2)}) collective-permute-start(bf16[32,128]{1,0:T(8,128)(2,1)S(1)} %get-tuple-element.25), channel_id=1, source_target_pairs={{0,16},{16,32},{32,48},{48,64},{64,80},{80,96},{96,112},{112,0},{1... | collective-permute-start | bytes 24584 | tf_op jit(solution)/shard_map/ppermute | solution.py:203
  22.5 5.4 %collective-permute-start.3 = (bf16[32,128]{1,0:T(8,128)(2,1)S(1)}, bf16[32,128]{1,0:T(8,128)(2,1)S(1)}, u32[]{:S(2)}, u32[]{:S(2)}) collective-permute-start(bf16[32,128]{1,0:T(8,128)(2,1)S(1)} %get-tuple-element.26), channel_id=1, source_target_pairs={{0,112},{16,0},{32,16},{48,32},{64,48},{80,64},{96,80},{112,96},{1... | collective-permute-start | bytes 24584 | tf_op jit(solution)/shard_map/ppermute | solution.py:203
  27.8 34.7 %copy-start.1 = (s32[16]{0:T(128)S(1)}, s32[16]{0:T(128)}, u32[]{:S(2)}) copy-start(s32[16]{0:T(128)} %order.1) | copy-start | bytes 196

commit v5 on v4

--- a/solution.py
+++ b/solution.py
@@ -110,14 +110,20 @@
 
 def shade_kernel(
     tf, middle_rows, weights, alpha, near, zlo, zhi, ylo, yhi, xlo, xhi, out, field, ends,
-    *, count, step_rows
+    sides, first_layer, last_layer, *, count, step_rows
 ):
     del middle_rows
     layers, rows, cols = weights.shape
     f32 = jnp.float32
     sub = iota((layers, 8, cols), 1)
-    kept = {axis: (near[2 * i : 2 * i + 1, :], near[2 * i + 1 : 2 * i + 2, :]) for i, axis in enumerate(AXES)}
-    low, high = kept["ty"]
+    kept = [(near[2 * i : 2 * i + 1, :], near[2 * i + 1 : 2 * i + 2, :]) for i in range(len(AXES))]
+    low, high = kept[0]
+    even = iota((rows, cols), 1) % 2 == 0
+    sides[...] = jnp.where(even, xhi[...].astype(f32) * high, xlo[...].astype(f32) * low)
+    low, high = kept[2]
+    first_layer[...] = zlo[...].astype(f32) * low
+    last_layer[...] = zhi[...].astype(f32) * high
+    low, high = kept[1]
     field[:, 0:8, :] = jnp.where(sub == 7, (ylo[...].astype(f32) * low)[:, None, :], 0.0)
     field[:, rows + 8 : rows + 16, :] = jnp.where(
         sub == 0, (yhi[...].astype(f32) * high)[:, None, :], 0.0
@@ -133,18 +139,14 @@
         base = pl.multiple_of(i * step_rows, step_rows)
         here = pl.ds(base, step_rows)
         middle = pl.ds(pl.multiple_of(base + 8, 8), step_rows)
-        low, high = kept["tx"]
-        sides = jnp.where(
-            lane % 2 == 0, xhi[here, :].astype(f32) * high, xlo[here, :].astype(f32) * low
-        )
+        around = sides[here, :]
         for k in range(layers):
-            ends[k] = sides if k == 0 else pltpu.roll(sides, cols - 2 * k, 1)
+            ends[k] = around if k == 0 else pltpu.roll(around, cols - 2 * k, 1)
         zero = jnp.zeros((step_rows, cols), f32)
         shaded, tints = (zero, [zero, zero, zero])
-        low, high = kept["depth"]
-        below, value = (zlo[here, :].astype(f32) * low, field[0, middle, :])
+        below, value = (first_layer[here, :], field[0, middle, :])
         for k in range(layers):
-            above = field[k + 1, middle, :] if k + 1 < layers else zhi[here, :].astype(f32) * high
+            above = field[k + 1, middle, :] if k + 1 < layers else last_layer[here, :]
             right = pltpu.roll(jnp.where(first_lane, ends[k], value), cols - 1, 1)
             left = pltpu.roll(jnp.where(last_lane, ends[k], value), 1, 1)
             sx, sz = (right - left, above - below)
@@ -270,7 +272,7 @@
         out_shape=[shape((count, 2, share, cols), jnp.int32), shape(field.shape, f32)],
         in_specs=[smem] + [vmem] * 10,
         out_specs=[vmem] * 2,
-        scratch_shapes=[VMEM((layers, step_rows, cols), f32)],
+        scratch_shapes=[VMEM((layers, step_rows, cols), f32)] + [VMEM((rows, cols), f32)] * 3,
         input_output_aliases={1: 1},
         compiler_params=limit,
         cost_estimate=pl.CostEstimate(

time: 88.4 us -> 88.2 us (level)
  no operation moved by 1% of the time
where the time goes in v5:
time: 88.2 us; the launch traced here: 87.9 us
  blocking collectives  51 us (58%)
  starting transfers between devices  21.9 us (25%)
  Pallas kernels  13.6 us (15%)
  waiting for transfers between devices  1.21 us (1%)
    all_to_all x2, blocking collectives, shards(): lax.all_to_all(words, 'depth', split_axis=0, concat_axis=0, tiled=True)  51 us
    ppermute x6, starting transfers between devices, halo(): lax.ppermute(array, axis, [(i, (i + shift) % count) for i in range(count)])  21.9 us
    pallas_call x1, Pallas kernels, shards(): pl.pallas_call(lambda *refs: shade_kernel(*refs, count=count, step_rows=s...  7.44 us
    pallas_call x1, Pallas kernels, shards(): pl.pallas_call(lambda *refs: absorb_kernel(*refs, count=count, step_rows=...  2.39 us
    pallas_call x1, Pallas kernels, shards(): pl.pallas_call(open_kernel, out_shape=[whole] * 3 + [shape((layers, rows...  2.17 us
  transfers between devices with their start and end apart: 6, of which 1 were waited for; matrix products, arithmetic and copies ran while one was open for 0% of the time, Pallas kernels for 3%

profile of v5, /device:TPU:6, one launch (start us, length us, event | category | flops | bytes accessed | tf_op | source)
XLA Modules:
  0.0 87.9 jit_solution(12656421948540969061)
XLA Ops:
  0.0 0.0 copy-start.2
  0.0 0.0 copy-start
  0.0 2.2 %open.1 = (bf16[256,128]{1,0:T(8,128)(2,1)S(1)}, bf16[256,128]{1,0:T(8,128)(2,1)S(1)}, bf16[256,128]{1,0:T(8,128)(2,1)S(1)}, f32[32,272,128]{2,1,0:T(8,128)S(1)}...) custom-call(bf16[32,256,128]{2,1,0:T(8,128)(2,1)} %volume.1, s32[256,128]{1,0:T(8,128)} %bitcast.7, ...), custom_call_target="tpu_custom_call" | custom-call | tf_op jit(solution)/shard_map/open/pallas_call | solution.py:235
  2.2 3.8 %collective-permute-start = (bf16[256,128]{1,0:T(8,128)(2,1)S(1)}, bf16[256,128]{1,0:T(8,128)(2,1)S(1)}, u32[]{:S(2)}, u32[]{:S(2)}) collective-permute-start(bf16[256,128]{1,0:T(8,128)(2,1)S(1)} %get-tuple-element.23), channel_id=1, source_target_pairs={{0,1},{1,2},{2,3},{3,4},{4,5},{5,6},{6,7},{7,8},{8,9},{9,10},{10,1... | collective-permute-start | bytes 196616 | tf_op jit(solution)/shard_map/ppermute | solution.py:205
  6.0 9.5 %collective-permute-start.1 = (bf16[256,128]{1,0:T(8,128)(2,1)S(1)}, bf16[256,128]{1,0:T(8,128)(2,1)S(1)}, u32[]{:S(2)}, u32[]{:S(2)}) collective-permute-start(bf16[256,128]{1,0:T(8,128)(2,1)S(1)} %get-tuple-element.24), channel_id=1, source_target_pairs={{0,15},{1,0},{2,1},{3,2},{4,3},{5,4},{6,5},{7,6},{8,7},{9,8},{10,9... | collective-permute-start | bytes 196616 | tf_op jit(solution)/shard_map/ppermute | solution.py:205
  15.5 4.9 %collective-permute-start.5 = (bf16[256,128]{1,0:T(8,128)(2,1)S(1)}, bf16[256,128]{1,0:T(8,128)(2,1)S(1)}, u32[]{:S(2)}, u32[]{:S(2)}) collective-permute-start(bf16[256,128]{1,0:T(8,128)(2,1)S(1)} %get-tuple-element.27), channel_id=1, source_target_pairs={{0,384},{128,0},{256,128},{384,256},{1,385},{129,1},{257,129},{385... | collective-permute-start | bytes 196616 | tf_op jit(solution)/shard_map/ppermute | solution.py:205
  20.5 1.9 %collective-permute-start.4 = (bf16[256,128]{1,0:T(8,128)(2,1)S(1)}, bf16[256,128]{1,0:T(8,128)(2,1)S(1)}, u32[]{:S(2)}, u32[]{:S(2)}) collective-permute-start(bf16[256,128]{1,0:T(8,128)(2,1)S(1)} %get-tuple-element.27), channel_id=1, source_target_pairs={{0,128},{128,256},{256,384},{384,0},{1,129},{129,257},{257,385},{3... | collective-permute-start | bytes 196616 | tf_op jit(solution)/shard_map/ppermute | solution.py:205
  22.4 0.0 collective-permute-done.arrived.refs_5_
  22.4 0.0 collective-permute-start.2
  22.5 1.7 %collective-permute-start.3 = (bf16[32,128]{1,0:T(8,128)(2,1)S(1)}, bf16[32,128]{1,0:T(8,128)(2,1)S(1)}, u32[]{:S(2)}, u32[]{:S(2)}) collective-permute-start(bf16[32,128]{1,0:T(8,128)(2,1)S(1)} %get-tuple-element.26), channel_id=1, source_target_pairs={{0,112},{16,0},{32,16},{48,32},{64,48},{80,64},{96,80},{112,96},{1... | collective-permute-start | bytes 24584 | tf_op jit(solution)/shard_map/ppermute | solution.py:205
  24.2 0.0 copy-done.2
  24.2 0.0 copy-done
  24.2 2.4 %absorb.1 = (f32[32,256,128]{2,1,0:T(8,128)S(1)}, f32[256,128]{1,0:T(8,128)S(1)}) custom-call(f32[2,4]{1,0:T(2,128)S(1)} %bitcast.4, s32[32]{0:T(128)S(1)} %bitcast.6, f32[32,272,128]{2,1,0:T(8,128)S(1)} %get-tuple-element.17.refs_2_.field.refs_1_, s32[256,128]{1,0:T(8,128)S(1)} %get-tuple-element.18.refs_3_, s32[256,128]{1,0:T(8,128)S(1)} %get-tuple-element.19.refs_4_), custom_call_target="tpu_custom_call" | custom-call | flops 12582912 | bytes 8388608 | tf_op jit(solution)/shard_map/absorb/pallas_call | solution.py:259
  26.6 0.0 collective-permute-done.1.refs_6_
  26.6 0.0 collective-permute-done.5.refs_10_
  26.6 1.2 %collective-permute-done.4.refs_9_ = bf16[256,128]{1,0:T(8,128)(2,1)S(1)} collective-permute-done((bf16[256,128]{1,0:T(8,128)(2,1)S(1)}, bf16[256,128]{1,0:T(8,128)(2,1)S(1)}, u32[]{:S(2)}, u32[]{:S(2)}) %collective-permute-start.4) | collective-permute-done | bytes 65568 | tf_op jit(solution)/shard_map/ppermute | solution.py:205
  27.8 0.0 collective-permute-done.2.refs_7_
  27.8 0.0 collective-permute-done.3.refs_8_
  27.8 7.4 %shade.1 = (s32[16,2,16,128]{3,2,1,0:T(8,128)S(1)}, f32[32,272,128]{2,1,0:T(8,128)S(1)}) custom-call(f32[2,4]{1,0:T(2,128)S(1)} %bitcast.5, f32[32,272,128]{2,1,0:T(8,128)S(1)} %get-tuple-element.17.refs_2_.field.refs_1_, f32[32,256,128]{2,1,0:T(8,128)S(1)} %get-tuple-element.20.refs_2_, ...), custom_call_target="tpu_custom_call", output_to_operand_aliasing={{1}: (1, {})} | custom-call | flops 41943040 | bytes 8388608 | tf_op jit(solution)/shard_map/shade/pallas_call | solution.py:270
  35.3 27.1 %all_to_all.10.parts = s32[16,2,16,128]{3,2,1,0:T(8,128)S(1)} all-to-all(s32[16,2,16,128]{3,2,1,0:T(8,128)S(1)} %get-tuple-element.28), channel_id=1, replica_groups=mesh['tx'=4,'ty'=8,'depth'=16] {'depth'}, dimensions={0} | all-to-all | bytes 524288 | tf_op jit(solution)/shard_map/all_to_all | solution.py:284
  62.4 0.0 copy-done.1
  62.4 0.7 composite.1
  63.1 23.9 %all_to_all.11.words = s32[16,2,16,128]{3,2,1,0:T(8,128)S(1)} all-to-all(s32[16,2,16,128]{3,2,1,0:T(8,128)S(1)} %composite.1), channel_id=1, replica_groups=mesh['tx'=4,'ty'=8,'depth'=16] {'depth'}, dimensions={0} | all-to-all | bytes 524288 | tf_op jit(solution)/shard_map/all_to_all | solution.py:293
  87.0 0.9 %frame.1 = f32[4,256,128]{2,1,0:T(8,128)} custom-call(s32[16,2,16,128]{3,2,1,0:T(8,128)S(1)} %all_to_all.11.words), custom_call_target="tpu_custom_call" | custom-call | tf_op jit(solution)/shard_map/frame/pallas_call | solution.py:294
  (2 shorter events, 0.0 us)
Async XLA Ops:
  0.0 24.2 %copy-start.2 = (s32[1,32,1]{1,2,0:T(1,128)S(1)}, s32[1,32,1]{1,2,0:T(1,128)}, u32[]{:S(2)}) copy-start(s32[1,32,1]{1,2,0:T(1,128)} %param.10) | copy-start | bytes 388
  0.0 24.2 %copy-start = (f32[4,2]{0,1:T(2,128)S(1)}, f32[4,2]{0,1:T(2,128)}, u32[]{:S(2)}) copy-start(f32[4,2]{0,1:T(2,128)} %param.7) | copy-start | bytes 100
  2.2 20.2 %collective-permute-start = (bf16[256,128]{1,0:T(8,128)(2,1)S(1)}, bf16[256,128]{1,0:T(8,128)(2,1)S(1)}, u32[]{:S(2)}, u32[]{:S(2)}) collective-permute-start(bf16[256,128]{1,0:T(8,128)(2,1)S(1)} %get-tuple-element.23), channel_id=1, source_target_pairs={{0,1},{1,2},{2,3},{3,4},{4,5},{5,6},{6,7},{7,8},{8,9},{9,10},{10,1... | collective-permute-start | bytes 196616 | tf_op jit(solution)/shard_map/ppermute | solution.py:205
  6.0 20.6 %collective-permute-start.1 = (bf16[256,128]{1,0:T(8,128)(2,1)S(1)}, bf16[256,128]{1,0:T(8,128)(2,1)S(1)}, u32[]{:S(2)}, u32[]{:S(2)}) collective-permute-start(bf16[256,128]{1,0:T(8,128)(2,1)S(1)} %get-tuple-element.24), channel_id=1, source_target_pairs={{0,15},{1,0},{2,1},{3,2},{4,3},{5,4},{6,5},{7,6},{8,7},{9,8},{10,9... | collective-permute-start | bytes 196616 | tf_op jit(solution)/shard_map/ppermute | solution.py:205
  15.5 11.1 %collective-permute-start.5 = (bf16[256,128]{1,0:T(8,128)(2,1)S(1)}, bf16[256,128]{1,0:T(8,128)(2,1)S(1)}, u32[]{:S(2)}, u32[]{:S(2)}) collective-permute-start(bf16[256,128]{1,0:T(8,128)(2,1)S(1)} %get-tuple-element.27), channel_id=1, source_target_pairs={{0,384},{128,0},{256,128},{384,256},{1,385},{129,1},{257,129},{385... | collective-permute-start | bytes 196616 | tf_op jit(solution)/shard_map/ppermute | solution.py:205
  20.5 7.4 %collective-permute-start.4 = (bf16[256,128]{1,0:T(8,128)(2,1)S(1)}, bf16[256,128]{1,0:T(8,128)(2,1)S(1)}, u32[]{:S(2)}, u32[]{:S(2)}) collective-permute-start(bf16[256,128]{1,0:T(8,128)(2,1)S(1)} %get-tuple-element.27), channel_id=1, source_target_pairs={{0,128},{128,256},{256,384},{384,0},{1,129},{129,257},{257,385},{3... | collective-permute-start | bytes 196616 | tf_op jit(solution)/shard_map/ppermute | solution.py:205
  22.4 5.4 %collective-permute-start.2 = (bf16[32,128]{1,0:T(8,128)(2,1)S(1)}, bf16[32,128]{1,0:T(8,128)(2,1)S(1)}, u32[]{:S(2)}, u32[]{:S(2)}) collective-permute-start(bf16[32,128]{1,0:T(8,128)(2,1)S(1)} %get-tuple-element.25), channel_id=1, source_target_pairs={{0,16},{16,32},{32,48},{48,64},{64,80},{80,96},{96,112},{112,0},{1... | collective-permute-start | bytes 24584 | tf_op jit(solution)/shard_map/ppermute | solution.py:205
  22.5 5.4 %collective-permute-start.3 = (bf16[32,128]{1,0:T(8,128)(2,1)S(1)}, bf16[32,128]{1,0:T(8,128)(2,1)S(1)}, u32[]{:S(2)}, u32[]{:S(2)}) collective-permute-start(bf16[32,128]{1,0:T(8,128)(2,1)S(1)} %get-tuple-element.26), channel_id=1, source_target_pairs={{0,112},{16,0},{32,16},{48,32},{64,48},{80,64},{96,80},{112,96},{1... | collective-permute-start | bytes 24584 | tf_op jit(solution)/shard_map/ppermute | solution.py:205
  27.8 34.6 %copy-start.1 = (s32[16]{0:T(128)S(1)}, s32[16]{0:T(128)}, u32[]{:S(2)}) copy-start(s32[16]{0:T(128)} %order.1) | copy-start | bytes 196
